TPU v7x, 128 devices: a whole 4x4x4 slice. The times are simulated.
128 devices in a mesh: head: 4 (over x), inner: 8 (over y, z_hi), outer: 4 (over z_lo, core).
Axes of the slice: x: 4, y: 4, z: 4 (z_hi: 2, z_lo: 2; z = z_hi * 2 + z_lo), core: 2. Of those that a mesh axis runs over, the one named last changes fastest.
Arguments:
- query_rows: bfloat16 [32, 4, 128, 1024], P(('inner', 'outer'), 'head'), may hold values from -6 to 6
- key_rows: bfloat16 [32, 4, 128, 256], P(('inner', 'outer'), 'head'), may hold values from -6 to 6
- value_rows: bfloat16 [32, 4, 128, 256], P(('inner', 'outer'), 'head'), may hold values from -6 to 6
- out_grad: bfloat16 [32, 4, 128, 1024], P(('inner', 'outer'), 'head'), may hold values from -6 to 6
- lengths: int32 [4], replicated, may hold values from 1 to 12288, 16384 in all
Outputs:
- attended: bfloat16 [32, 4, 128, 1024], P(('inner', 'outer'), 'head')
- query_grad: bfloat16 [32, 4, 128, 1024], P(('inner', 'outer'), 'head')
- key_grad: bfloat16 [32, 4, 128, 256], P(('inner', 'outer'), 'head')
- value_grad: bfloat16 [32, 4, 128, 256], P(('inner', 'outer'), 'head')
Inputs may be any that keep to these rules, and one draw needn't show every extreme that they name: The 4 lengths sum to 16384; the largest is exactly 12288.
All inputs are finite; a program needn't handle non-finite values.
Results may differ from a plain program's by a relative error of at most 0.03.
Values may be sent and summed in bfloat16 or wider, within the bound.
No kernel may reach another device: no remote copies, remote signals or barrier semaphores. Data moves between devices by JAX's collectives and lax.ppermute only.
A program may use at most 64 MiB of HBM per device.

v0:
```python
import jax
import jax.numpy as jnp
from jax import lax
from jax.experimental import pallas as pl
from jax.experimental.pallas import tpu as pltpu
from jax.sharding import Mesh
from jax.sharding import PartitionSpec as P

HD = 128
NEG = -1.0e30
SCALE = HD ** -0.5
SC2 = SCALE * 1.4426950408889634
QT = 16
KP = 16
LIST = 160
bf16, f32, i32 = jnp.bfloat16, jnp.float32, jnp.int32
VMEM = pl.BlockSpec(memory_space=pltpu.VMEM)
SMEM = pl.BlockSpec(memory_space=pltpu.SMEM)


def nt(a, b):
    return lax.dot_general(a, b, (((1,), (1,)), ((), ())), preferred_element_type=f32)


def nn(a, b):
    return jnp.dot(a, b, preferred_element_type=f32)


def head_rows(ref, n, first):
    block = ref[:, n].reshape(64, ref.shape[-1])
    return jnp.concatenate([block[:, first + h * HD:first + (h + 1) * HD] for h in range(4)], axis=0)


def list_steps(plan_ref, plain, edge):
    def outer(d, counts):
        def inner(n, counts):
            a, b = counts
            p = n - d
            plain[a] = n * 256 + p
            edge[b] = n * 256 + p
            is_plain = ((p >= plan_ref[1, n]) & (d > 0)).astype(i32)
            is_live = (p >= plan_ref[0, n]).astype(i32)
            return a + is_plain, b + is_live * (1 - is_plain)

        return lax.fori_loop(d, QT, inner, counts)

    counts = lax.fori_loop(0, QT, outer, (jnp.int32(0), jnp.int32(0)))
    for i in range(8):
        plain[counts[0] + i] = QT * 256
        edge[counts[1] + i] = QT * 256
    return counts


def unpack(steps, t):
    word = steps[t]
    return word // 256, word % 256


def visible(p, n, offset, pos_ref):
    r = lax.broadcasted_iota(i32, (256, 1), 0)
    kpos = p * 1024 + (r // 32) * 128 + offset + r % 32
    return (kpos <= pos_ref[n, 0:1, :]) & (kpos >= pos_ref[n, 1:2, :])


def keys_at(ref, p):
    return ref[pl.ds(pl.multiple_of(p * 256, 256), 256), :]


def lanes_at(ref, p):
    return ref[:, pl.ds(pl.multiple_of(p * 256, 256), 256)]


def sort_keys(core, own_ref, oth_ref, first, put):
    @pl.loop(0, KP)
    def _(m):
        own = own_ref[:, m].reshape(128, 2 * HD)[:, first:first + HD]
        oth = oth_ref[:, m].reshape(128, 2 * HD)[:, first:first + HD]
        put(2 * m + core, own)
        put(2 * m + 1 - core, oth)


def put_rows(ref):
    def put(c, rows):
        ref[pl.ds(pl.multiple_of(c * 128, 128), 128), :] = rows
    return put


def put_lanes(ref):
    def put(c, rows):
        ref[:, pl.ds(pl.multiple_of(c * 128, 128), 128)] = rows.T
    return put


def fwd_kernel(plan_ref, pos_ref, qd_ref, own_ref, oth_ref, ot_ref, st_ref,
               q_s, k_s, vt, m_s, l_s, acc, s_buf, p_buf, a_buf, plain, edge):
    core, offset = plan_ref[2, 0], plan_ref[2, 1]
    counts = list_steps(plan_ref, plain, edge)
    sort_keys(core, own_ref, oth_ref, 0, put_rows(k_s))
    sort_keys(core, own_ref, oth_ref, HD, put_lanes(vt))

    @pl.loop(0, QT)
    def _(n):
        q_s[n] = head_rows(qd_ref, n, 0)
    q_s[QT] = jnp.zeros((256, HD), bf16)
    m_s[...] = jnp.full_like(m_s, NEG)
    l_s[...] = jnp.zeros_like(l_s)
    acc[...] = jnp.zeros_like(acc)

    def run(steps, count, masked):
        def score(t, buf):
            n, p = unpack(steps, t)
            s = nt(keys_at(k_s, p), q_s[n]) * SC2
            if masked:
                s = jnp.where(visible(p, n, offset, pos_ref), s, 2 * NEG)
            s_buf[buf] = s

        def soften(t, buf):
            n, _ = unpack(steps, t)
            s = s_buf[buf]
            old = m_s[n]
            new = jnp.maximum(old, jnp.max(s, axis=0, keepdims=True))
            w = jnp.exp2(s - new)
            alpha = jnp.exp2(old - new)
            m_s[n] = new
            l_s[n] = l_s[n] * alpha + jnp.sum(w, axis=0, keepdims=True)
            a_buf[buf] = alpha
            p_buf[buf] = w.astype(bf16)

        def gather(t, buf):
            n, p = unpack(steps, t)
            acc[n] = acc[n] * a_buf[buf] + nn(lanes_at(vt, p), p_buf[buf])

        p_buf[2] = jnp.zeros((256, 256), bf16)
        p_buf[3] = jnp.zeros((256, 256), bf16)
        a_buf[2] = jnp.ones((1, 256), f32)
        a_buf[3] = jnp.ones((1, 256), f32)
        score(0, 0)
        score(1, 1)
        trips = (count + 3) // 4

        @pl.loop(0, trips)
        def _(i):
            t = 4 * i
            for half in (0, 2):
                cur, nxt = half, 2 - half
                for k in (0, 1):
                    score(t + half + 2 + k, nxt + k)
                for k in (0, 1):
                    gather(jnp.maximum(t + half - 2 + k, 0), nxt + k)
                for k in (0, 1):
                    soften(t + half + k, cur + k)

        last = jnp.maximum(4 * trips - 2, 0)
        gather(last, 2)
        gather(last + 1, 3)

    run(plain, counts[0], False)
    run(edge, counts[1], True)

    @pl.loop(0, QT)
    def _(n):
        o = acc[n]
        ot_ref[n] = o
        st_ref[n, 0:1, :] = m_s[n]
        st_ref[n, 1:2, :] = l_s[n]
        st_ref[n, 2:3, :] = jnp.sum(head_rows(qd_ref, n, 512).astype(f32).T * o, axis=0, keepdims=True)


def bwd_kernel(plan_ref, pos_ref, st0_ref, st1_ref, st2_ref, st3_ref, qd_ref, own_ref, oth_ref, ot_ref,
               oq_ref, down_ref, doth_ref,
               q_s, do_s, k_s, v_s, kt, lse_s, delta_s, w_s, dq, dk, dv, s_buf, dp_buf, p_buf, ds_buf, plain, edge):
    core, offset = plan_ref[2, 0], plan_ref[2, 1]
    counts = list_steps(plan_ref, plain, edge)
    sort_keys(core, own_ref, oth_ref, 0, put_rows(k_s))
    sort_keys(core, own_ref, oth_ref, HD, put_rows(v_s))
    sort_keys(core, own_ref, oth_ref, 0, put_lanes(kt))
    refs = (st0_ref, st1_ref, st2_ref, st3_ref)

    @pl.loop(0, QT)
    def _(n):
        q_s[n] = head_rows(qd_ref, n, 0)
        do_s[n] = head_rows(qd_ref, n, 512)
        top = refs[0][n, 0:1, :]
        for ref in refs[1:]:
            top = jnp.maximum(top, ref[n, 0:1, :])
        share = [jnp.exp2(ref[n, 0:1, :] - top) for ref in refs]
        total = sum(w * ref[n, 1:2, :] for w, ref in zip(share, refs))
        lse_s[n] = top + jnp.log2(total)
        delta_s[n] = sum(w * ref[n, 2:3, :] for w, ref in zip(share, refs)) / total
        w_s[n] = share[0] / total
    q_s[QT] = jnp.zeros((256, HD), bf16)
    do_s[QT] = jnp.zeros((256, HD), bf16)
    lse_s[QT] = jnp.zeros((1, 256), f32)
    delta_s[QT] = jnp.zeros((1, 256), f32)
    dq[...] = jnp.zeros_like(dq)
    dk[...] = jnp.zeros_like(dk)
    dv[...] = jnp.zeros_like(dv)

    def run(steps, count, masked):
        def score(t, buf):
            n, p = unpack(steps, t)
            s = nt(keys_at(k_s, p), q_s[n]) * SC2
            if masked:
                s = jnp.where(visible(p, n, offset, pos_ref), s, NEG)
            s_buf[buf] = s
            dp_buf[buf] = nt(keys_at(v_s, p), do_s[n])

        def soften(t, buf):
            n, _ = unpack(steps, t)
            w = jnp.exp2(s_buf[buf] - lse_s[n])
            p_buf[buf] = w.astype(bf16)
            ds_buf[buf] = (w * (dp_buf[buf] - delta_s[n])).astype(bf16)

        def gather(t, buf):
            n, p = unpack(steps, t)
            rows = pl.ds(pl.multiple_of(p * 256, 256), 256)
            ds = ds_buf[buf]
            dv[rows, :] += nn(p_buf[buf], do_s[n])
            dk[rows, :] += nn(ds, q_s[n])
            dq[n] += nn(lanes_at(kt, p), ds)

        for buf in (2, 3):
            p_buf[buf] = jnp.zeros((256, 256), bf16)
            ds_buf[buf] = jnp.zeros((256, 256), bf16)
        score(0, 0)
        score(1, 1)
        trips = (count + 3) // 4

        @pl.loop(0, trips)
        def _(i):
            t = 4 * i
            for half in (0, 2):
                cur, nxt = half, 2 - half
                for k in (0, 1):
                    score(t + half + 2 + k, nxt + k)
                for k in (0, 1):
                    gather(jnp.maximum(t + half - 2 + k, 0), nxt + k)
                for k in (0, 1):
                    soften(t + half + k, cur + k)

        last = jnp.maximum(4 * trips - 2, 0)
        gather(last, 2)
        gather(last + 1, 3)

    run(plain, counts[0], False)
    run(edge, counts[1], True)

    @pl.loop(0, QT)
    def _(n):
        ob = (ot_ref[n] * w_s[n]).T.astype(bf16)
        qb = (dq[n] * SCALE).T.astype(bf16)
        for h in range(4):
            oq_ref[:, n, :, h * HD:(h + 1) * HD] = ob[h * 64:(h + 1) * 64].reshape(4, 16, HD)
            oq_ref[:, n, :, 512 + h * HD:512 + (h + 1) * HD] = qb[h * 64:(h + 1) * 64].reshape(4, 16, HD)

    @pl.loop(0, KP)
    def _(m):
        for ref, c in ((down_ref, 2 * m + core), (doth_ref, 2 * m + 1 - core)):
            rows = pl.ds(pl.multiple_of(c * 128, 128), 128)
            ref[:, m, :, :HD] = (dk[rows, :] * SCALE).astype(bf16).reshape(4, 32, HD)
            ref[:, m, :, HD:] = dv[rows, :].astype(bf16).reshape(4, 32, HD)


def fwd(plan, pos, qd, own, oth):
    return pl.pallas_call(
        fwd_kernel,
        in_specs=[SMEM, VMEM, VMEM, VMEM, VMEM],
        out_specs=[VMEM, VMEM],
        scratch_shapes=[
            pltpu.VMEM((QT + 1, 256, HD), bf16), pltpu.VMEM((KP * 256, HD), bf16), pltpu.VMEM((HD, KP * 256), bf16),
            pltpu.VMEM((QT + 1, 1, 256), f32), pltpu.VMEM((QT + 1, 1, 256), f32), pltpu.VMEM((QT + 1, HD, 256), f32),
            pltpu.VMEM((4, 256, 256), f32), pltpu.VMEM((4, 256, 256), bf16), pltpu.VMEM((4, 1, 256), f32),
            pltpu.SMEM((LIST,), i32), pltpu.SMEM((LIST,), i32),
        ],
        out_shape=[jax.ShapeDtypeStruct((QT, HD, 256), f32), jax.ShapeDtypeStruct((QT, 4, 256), f32)],
        compiler_params=pltpu.CompilerParams(vmem_limit_bytes=40 << 20),
        name="fwd",
    )(plan, pos, qd, own, oth)


def bwd(plan, pos, sts, qd, own, oth, ot):
    half = jax.ShapeDtypeStruct((4, KP, 32, 2 * HD), bf16)
    return pl.pallas_call(
        bwd_kernel,
        in_specs=[SMEM] + [VMEM] * 9,
        out_specs=[VMEM] * 3,
        scratch_shapes=[
            pltpu.VMEM((QT + 1, 256, HD), bf16), pltpu.VMEM((QT + 1, 256, HD), bf16),
            pltpu.VMEM((KP * 256, HD), bf16), pltpu.VMEM((KP * 256, HD), bf16), pltpu.VMEM((HD, KP * 256), bf16),
            pltpu.VMEM((QT + 1, 1, 256), f32), pltpu.VMEM((QT + 1, 1, 256), f32), pltpu.VMEM((QT + 1, 1, 256), f32),
            pltpu.VMEM((QT + 1, HD, 256), f32), pltpu.VMEM((KP * 256, HD), f32), pltpu.VMEM((KP * 256, HD), f32),
            pltpu.VMEM((4, 256, 256), f32), pltpu.VMEM((4, 256, 256), f32),
            pltpu.VMEM((4, 256, 256), bf16), pltpu.VMEM((4, 256, 256), bf16),
            pltpu.SMEM((LIST,), i32), pltpu.SMEM((LIST,), i32),
        ],
        out_shape=[jax.ShapeDtypeStruct((4, QT, 16, 1024), bf16), half, half],
        compiler_params=pltpu.CompilerParams(vmem_limit_bytes=48 << 20),
        name="bwd",
    )(plan, pos, *sts, qd, own, oth, ot)


def make_plan(lengths, core, u, j):
    n = jnp.arange(QT + 1, dtype=i32)[:, None, None]
    x = jnp.arange(4, dtype=i32)[None, :, None]
    t = jnp.arange(16, dtype=i32)[None, None, :]
    pos = (512 * (2 * n + core) + 128 * x + 16 * u + t).reshape(QT + 1, 64)
    ends = jnp.cumsum(lengths)
    start = jnp.sum(jnp.where(ends[None, None, :] <= pos[:, :, None], lengths, 0), axis=-1)
    low = start[:QT, 0] // 1024
    plain = (start[:QT, -1] + 1023) // 1024
    extra = jnp.zeros((QT,), i32).at[0].set(core).at[1].set(32 * j)
    plan = jnp.stack([low, plain, extra]).astype(i32)
    rows = jnp.stack([jnp.tile(pos, (1, 4)), jnp.tile(start, (1, 4))], axis=1)
    return plan, rows.astype(i32)


PLANE = ("head", "inner", "zl")


def on_device(query_rows, key_rows, value_rows, out_grad, lengths):
    j, u, g, core = (lax.axis_index(name) for name in ("head", "inner", "zl", "core"))
    plan, pos = make_plan(lengths, core, u, j)
    swap = [(0, 1), (1, 0)]

    def send_keys(rows):
        return rows.reshape(4, 32, 2, HD).transpose(0, 2, 1, 3)

    kv = jnp.concatenate([send_keys(key_rows), send_keys(value_rows)], axis=-1)
    kv = jnp.broadcast_to(kv[:, None], (4, 8, 2, 32, 2 * HD)).reshape(64, 32, 2 * HD)
    own = lax.all_to_all(kv, PLANE, 0, 0, tiled=True)
    oth = lax.ppermute(own, "core", swap)

    def send_rows(rows):
        return rows.reshape(8, 16, 2, 512).transpose(0, 2, 1, 3)

    qd = jnp.concatenate([send_rows(query_rows), send_rows(out_grad)], axis=-1)
    qd = jnp.broadcast_to(qd[None], (4, 8, 2, 16, 1024)).reshape(64, 16, 1024)
    qd = lax.all_to_all(qd, PLANE, 0, 0, tiled=True).reshape(4, QT, 16, 1024)
    own, oth = own.reshape(4, KP, 32, 2 * HD), oth.reshape(4, KP, 32, 2 * HD)
    ot, st = fwd(plan, pos, qd, own, oth)
    sts = [st] + [lax.ppermute(st, "head", [(i, (i + k) % 4) for i in range(4)]) for k in (1, 2, 3)]
    oq, down, doth = bwd(plan, pos, sts, qd, own, oth, ot)
    other = lax.ppermute(doth, "core", swap)
    dkv = (down.astype(f32) + other.astype(f32)).astype(bf16).reshape(64, 32, 2 * HD)
    dkv = lax.all_to_all(dkv, PLANE, 0, 0, tiled=True).reshape(4, 8, 2, 32, 2, HD)
    dkv = jnp.sum(dkv.astype(f32), axis=1).astype(bf16)
    dkv = dkv.transpose(3, 0, 2, 1, 4).reshape(2, 1, 1, 128, 2 * HD)
    oq = lax.all_to_all(oq.reshape(64, 16, 1024), PLANE, 0, 0, tiled=True).reshape(4, 8, 2, 16, 2, 512)
    oq = jnp.sum(oq.astype(f32), axis=0).astype(bf16)
    oq = oq.transpose(3, 0, 2, 1, 4).reshape(2, 1, 1, 128, 1024)
    return oq[0], oq[1], dkv[0], dkv[1]


def solution(mesh):
    finer = Mesh(mesh.devices.reshape(4, 8, 2, 2), ("head", "inner", "zl", "core"))
    placed = P(("inner", "zl", "core"), "head", None, None)
    return jax.shard_map(
        on_device,
        mesh=finer,
        in_specs=(placed, placed, placed, placed, P()),
        out_specs=(placed, placed, placed, placed),
        check_vma=False,
    )
```

profile of v0, /device:TPU:0, one launch (start us, length us, event | category | flops | bytes accessed | tf_op | source)
XLA Modules:
  0.0 186.1 jit_solution(12352190739619417606)
XLA Ops:
  0.6 0.0 copy-start.2
  0.6 0.9 reshape.355
  1.5 0.9 reshape.356
  2.4 0.1 pad_maximum_fusion.1
  2.5 0.0 copy-start.3
  2.6 1.1 broadcast_in_dim.15
  3.7 11.5 %all-to-all-start.1 = ((bf16[64,32,256]{2,1,0:T(8,128)(2,1)}), bf16[64,32,256]{2,1,0:T(8,128)(2,1)S(1)}, u32[]{:S(2)}, u32[]{:S(2)}) async-start(bf16[64,32,256]{2,1,0:T(8,128)(2,1)} %bitcast.11), calls=%async_computation.1 | async-start | bytes 2097152 | tf_op jit(solution)/shard_map/all_to_all | solution.py:330
  15.2 0.0 copy-done.2
  15.2 0.2 reshape.351
  15.4 0.0 copy-done.3
  15.4 0.2 reshape.352
  15.6 0.5 pad_maximum_fusion
  16.1 0.1 copy.31
  16.2 17.5 %all-to-all-done.1 = bf16[64,32,256]{2,1,0:T(8,128)(2,1)S(1)} async-done(((bf16[64,32,256]{2,1,0:T(8,128)(2,1)}), bf16[64,32,256]{2,1,0:T(8,128)(2,1)S(1)}, u32[]{:S(2)}, u32[]{:S(2)}) %all-to-all-start.1) | async-done | bytes 1048608 | tf_op jit(solution)/shard_map/all_to_all | solution.py:330
  33.7 1.6 broadcast_in_dim.14
  35.4 0.0 copy-start.4
  35.4 4.8 %all-to-all-start = ((bf16[64,16,1024]{2,1,0:T(8,128)(2,1)}), bf16[64,16,1024]{2,1,0:T(8,128)(2,1)S(1)}, u32[]{:S(2)}, u32[]{:S(2)}) async-start(bf16[64,16,1024]{2,1,0:T(8,128)(2,1)} %bitcast.47), calls=%async_computation | async-start | bytes 4194304 | tf_op jit(solution)/shard_map/all_to_all | solution.py:338
  40.2 0.1 collective-permute-start
  40.3 0.1 add_add_fusion
  40.4 0.1 add.115
  40.5 0.1 add.112
  40.6 0.1 add.113
  40.6 0.0 copy-done.4
  40.7 0.2 reduce-window.8
  40.8 0.1 select_reduce_fusion
  41.0 0.1 tile.18
  41.1 0.1 tile.16
  41.2 0.1 scatter.9
  41.3 0.2 slice_reduce_fusion
  41.6 27.4 %all-to-all-done = bf16[64,16,1024]{2,1,0:T(8,128)(2,1)S(1)} async-done(((bf16[64,16,1024]{2,1,0:T(8,128)(2,1)}), bf16[64,16,1024]{2,1,0:T(8,128)(2,1)S(1)}, u32[]{:S(2)}, u32[]{:S(2)}) %all-to-all-start) | async-done | bytes 2097184 | tf_op jit(solution)/shard_map/all_to_all | solution.py:338
  69.0 0.0 copy-start
  69.0 0.0 collective-permute-done
  69.0 21.5 %fwd.1 = (f32[16,128,256]{2,1,0:T(8,128)S(1)}, f32[16,4,256]{2,1,0:T(4,128)S(1)}) custom-call(s32[3,16]{1,0:T(4,128)S(1)} %pad_add_fusion.1.plan_ref, s32[17,2,256]{2,1,0:T(2,128)S(1)} %pad_add_fusion.pos_ref, bf16[4,16,16,1024]{3,2,1,0:T(8,128)(2,1)S(1)} %bitcast.43, bf16[4,16,32,256]{3,2,1,0:T(8,128)(2,1)S(1)} %bitcast.45, ...), custom_call_target="tpu_custom_call" | custom-call | tf_op jit(solution)/shard_map/fwd/pallas_call | solution.py:265
  90.5 0.0 copy-done
  90.5 0.0 copy-start.1
  90.5 1.3 copy-done.1
  91.8 0.9 collective-permute-start.3
  92.7 1.2 collective-permute-start.2
  94.0 0.5 collective-permute-start.1
  94.5 1.6 collective-permute-done.3.st3_ref
  96.1 2.4 %collective-permute-done.2.st2_ref = f32[16,4,256]{2,1,0:T(4,128)S(1)} collective-permute-done((f32[16,4,256]{2,1,0:T(4,128)S(1)}, f32[16,4,256]{2,1,0:T(4,128)S(1)}, u32[]{:S(2)}, u32[]{:S(2)}) %collective-permute-start.2) | collective-permute-done | bytes 65568 | tf_op jit(solution)/shard_map/ppermute | solution.py:341
  98.5 0.9 collective-permute-done.1.st1_ref
  99.4 33.4 %bwd.1 = (bf16[4,16,16,1024]{3,2,1,0:T(8,128)(2,1)}, bf16[4,16,32,256]{3,2,1,0:T(8,128)(2,1)S(1)}, bf16[4,16,32,256]{3,2,1,0:T(8,128)(2,1)S(1)}) custom-call(s32[3,16]{1,0:T(4,128)S(1)} %pad_add_fusion.1.plan_ref, s32[17,2,256]{2,1,0:T(2,128)S(1)} %pad_add_fusion.pos_ref, f32[16,4,256]{2,1,0:T(4,128)S(1)} %get-tuple-element.33.st0_ref, ...), custom_call_target="tpu_custom_call" | custom-call | tf_op jit(solution)/shard_map/bwd/pallas_call | solution.py:283
  132.9 6.6 %all-to-all-start.2 = ((bf16[64,16,1024]{2,1,0:T(8,128)(2,1)}), bf16[64,16,1024]{2,1,0:T(8,128)(2,1)}, u32[]{:S(2)}, u32[]{:S(2)}) async-start(bf16[64,16,1024]{2,1,0:T(8,128)(2,1)} %bitcast.49), calls=%async_computation.2 | async-start | bytes 4194304 | tf_op jit(solution)/shard_map/all_to_all | solution.py:348
  139.4 0.3 collective-permute-start.4
  139.7 2.6 %collective-permute-done.4 = bf16[4,16,32,256]{3,2,1,0:T(8,128)(2,1)S(1)} collective-permute-done((bf16[4,16,32,256]{3,2,1,0:T(8,128)(2,1)S(1)}, bf16[4,16,32,256]{3,2,1,0:T(8,128)(2,1)S(1)}, u32[]{:S(2)}, u32[]{:S(2)}) %collective-permute-start.4) | collective-permute-done | bytes 1048608 | tf_op jit(solution)/shard_map/ppermute | solution.py:343
  142.4 1.4 add_convert_fusion
  143.8 17.0 %all-to-all-done.2 = bf16[64,16,1024]{2,1,0:T(8,128)(2,1)} async-done(((bf16[64,16,1024]{2,1,0:T(8,128)(2,1)}), bf16[64,16,1024]{2,1,0:T(8,128)(2,1)}, u32[]{:S(2)}, u32[]{:S(2)}) %all-to-all-start.2) | async-done | bytes 2097184 | tf_op jit(solution)/shard_map/all_to_all | solution.py:348
  160.8 5.7 %all-to-all-start.3 = ((bf16[64,32,256]{2,1,0:T(8,128)(2,1)}), bf16[64,32,256]{2,1,0:T(8,128)(2,1)}, u32[]{:S(2)}, u32[]{:S(2)}) async-start(bf16[64,32,256]{2,1,0:T(8,128)(2,1)} %bitcast.16), calls=%async_computation.3 | async-start | bytes 2097152 | tf_op jit(solution)/shard_map/all_to_all | solution.py:345
  166.5 3.3 %reshape.361 = bf16[4,8,2,16,2,512]{5,4,3,2,1,0:T(2,128)(2,1)S(1)} reshape(bf16[64,16,1024]{2,1,0:T(8,128)(2,1)} %all-to-all-done.2) | data formatting | bytes 4194304 | tf_op jit(solution)/shard_map/reshape | solution.py:348
  169.8 3.1 %reduce_sum.34 = bf16[8,2,16,2,512]{4,3,2,1,0:T(2,128)(2,1)S(1)} reduce(bf16[4,8,2,16,2,512]{5,4,3,2,1,0:T(2,128)(2,1)S(1)} %reshape.361, bf16[]{:T(256)} %constant.103.clone.1), dimensions={0}, to_apply=%region_2.3 | reduce | flops 786432 | bytes 2621442 | tf_op jit(solution)/shard_map/reduce_sum | solution.py:349
  173.0 0.8 fusion.1
  173.8 0.4 copy.34
  174.2 0.9 squeeze.18
  175.1 0.4 copy.33
  175.5 0.9 squeeze.17
  176.3 5.4 %all-to-all-done.3 = bf16[64,32,256]{2,1,0:T(8,128)(2,1)} async-done(((bf16[64,32,256]{2,1,0:T(8,128)(2,1)}), bf16[64,32,256]{2,1,0:T(8,128)(2,1)}, u32[]{:S(2)}, u32[]{:S(2)}) %all-to-all-start.3) | async-done | bytes 1048608 | tf_op jit(solution)/shard_map/all_to_all | solution.py:345
  181.7 1.3 reshape.363
  183.1 1.2 reduce_sum.35
  184.3 0.2 fusion.2
  184.6 0.1 copy.36
  184.7 0.7 squeeze.20
  185.4 0.1 copy.35
  185.5 0.7 squeeze.19
  (11 shorter events, 0.1 us)
Async XLA Ops:
  0.6 14.6 %copy-start.2 = (bf16[1,1,128,1024]{3,2,1,0:T(8,128)(2,1)S(1)}, bf16[1,1,128,1024]{3,2,1,0:T(8,128)(2,1)}, u32[]{:S(2)}) copy-start(bf16[1,1,128,1024]{3,2,1,0:T(8,128)(2,1)} %param.9) | copy-start | bytes 786436
  2.5 12.8 %copy-start.3 = (bf16[1,1,128,1024]{3,2,1,0:T(8,128)(2,1)S(1)}, bf16[1,1,128,1024]{3,2,1,0:T(8,128)(2,1)}, u32[]{:S(2)}) copy-start(bf16[1,1,128,1024]{3,2,1,0:T(8,128)(2,1)} %param.12) | copy-start | bytes 786436
  3.7 30.0 %all-to-all-start.1 = ((bf16[64,32,256]{2,1,0:T(8,128)(2,1)}), bf16[64,32,256]{2,1,0:T(8,128)(2,1)S(1)}, u32[]{:S(2)}, u32[]{:S(2)}) async-start(bf16[64,32,256]{2,1,0:T(8,128)(2,1)} %bitcast.11), calls=%async_computation.1 | async-start | bytes 2097152 | tf_op jit(solution)/shard_map/all_to_all | solution.py:330
  35.4 5.3 %copy-start.4 = (s32[4]{0:T(128)S(1)}, s32[4]{0:T(128)}, u32[]{:S(2)}) copy-start(s32[4]{0:T(128)} %param.13) | copy-start | bytes 52
  35.4 33.7 %all-to-all-start = ((bf16[64,16,1024]{2,1,0:T(8,128)(2,1)}), bf16[64,16,1024]{2,1,0:T(8,128)(2,1)S(1)}, u32[]{:S(2)}, u32[]{:S(2)}) async-start(bf16[64,16,1024]{2,1,0:T(8,128)(2,1)} %bitcast.47), calls=%async_computation | async-start | bytes 4194304 | tf_op jit(solution)/shard_map/all_to_all | solution.py:338
  40.2 28.8 %collective-permute-start = (bf16[64,32,256]{2,1,0:T(8,128)(2,1)S(1)}, bf16[64,32,256]{2,1,0:T(8,128)(2,1)}, u32[]{:S(2)}, u32[]{:S(2)}) collective-permute-start(bf16[64,32,256]{2,1,0:T(8,128)(2,1)S(1)} %all-to-all-done.1), channel_id=1, source_target_pairs={{0,1},{1,0},{2,3},{3,2},{4,5},{5,4},{6,7},{7,6},{8,9},{9,8},{10,11... | collective-permute-start | bytes 3145736 | tf_op jit(solution)/shard_map/ppermute | solution.py:331
  69.0 21.5 %copy-start = (bf16[64,16,1024]{2,1,0:T(8,128)(2,1)}, bf16[64,16,1024]{2,1,0:T(8,128)(2,1)S(1)}, u32[]{:S(2)}) copy-start(bf16[64,16,1024]{2,1,0:T(8,128)(2,1)S(1)} %all-to-all-done) | copy-start | bytes 6291460
  90.5 1.3 copy-start.1
  91.8 4.3 %collective-permute-start.3 = (f32[16,4,256]{2,1,0:T(4,128)S(1)}, f32[16,4,256]{2,1,0:T(4,128)S(1)}, u32[]{:S(2)}, u32[]{:S(2)}) collective-permute-start(f32[16,4,256]{2,1,0:T(4,128)S(1)} %get-tuple-element.33.st0_ref), channel_id=1, source_target_pairs={{0,96},{32,0},{64,32},{96,64},{1,97},{33,1},{65,33},{97,65},{2,98}... | collective-permute-start | bytes 196616 | tf_op jit(solution)/shard_map/ppermute | solution.py:341
  92.7 5.8 %collective-permute-start.2 = (f32[16,4,256]{2,1,0:T(4,128)S(1)}, f32[16,4,256]{2,1,0:T(4,128)S(1)}, u32[]{:S(2)}, u32[]{:S(2)}) collective-permute-start(f32[16,4,256]{2,1,0:T(4,128)S(1)} %get-tuple-element.33.st0_ref), channel_id=1, source_target_pairs={{0,64},{32,96},{64,0},{96,32},{1,65},{33,97},{65,1},{97,33},{2,66}... | collective-permute-start | bytes 196616 | tf_op jit(solution)/shard_map/ppermute | solution.py:341
  94.0 5.5 %collective-permute-start.1 = (f32[16,4,256]{2,1,0:T(4,128)S(1)}, f32[16,4,256]{2,1,0:T(4,128)S(1)}, u32[]{:S(2)}, u32[]{:S(2)}) collective-permute-start(f32[16,4,256]{2,1,0:T(4,128)S(1)} %get-tuple-element.33.st0_ref), channel_id=1, source_target_pairs={{0,32},{32,64},{64,96},{96,0},{1,33},{33,65},{65,97},{97,1},{2,34}... | collective-permute-start | bytes 196616 | tf_op jit(solution)/shard_map/ppermute | solution.py:341
  132.9 27.9 %all-to-all-start.2 = ((bf16[64,16,1024]{2,1,0:T(8,128)(2,1)}), bf16[64,16,1024]{2,1,0:T(8,128)(2,1)}, u32[]{:S(2)}, u32[]{:S(2)}) async-start(bf16[64,16,1024]{2,1,0:T(8,128)(2,1)} %bitcast.49), calls=%async_computation.2 | async-start | bytes 4194304 | tf_op jit(solution)/shard_map/all_to_all | solution.py:348
  139.4 2.9 %collective-permute-start.4 = (bf16[4,16,32,256]{3,2,1,0:T(8,128)(2,1)S(1)}, bf16[4,16,32,256]{3,2,1,0:T(8,128)(2,1)S(1)}, u32[]{:S(2)}, u32[]{:S(2)}) collective-permute-start(bf16[4,16,32,256]{3,2,1,0:T(8,128)(2,1)S(1)} %get-tuple-element.37), channel_id=1, source_target_pairs={{0,1},{1,0},{2,3},{3,2},{4,5},{5,4},{6,7},{7,6},{8,9},{9,8},{10,11... | collective-permute-start | bytes 3145736 | tf_op jit(solution)/shard_map/ppermute | solution.py:343
  160.8 20.9 %all-to-all-start.3 = ((bf16[64,32,256]{2,1,0:T(8,128)(2,1)}), bf16[64,32,256]{2,1,0:T(8,128)(2,1)}, u32[]{:S(2)}, u32[]{:S(2)}) async-start(bf16[64,32,256]{2,1,0:T(8,128)(2,1)} %bitcast.16), calls=%async_computation.3 | async-start | bytes 2097152 | tf_op jit(solution)/shard_map/all_to_all | solution.py:345
where the time goes:
time: 187 us; the launch traced here: 186 us
  waiting for transfers between devices  75 us (40%)
  Pallas kernels  54.9 us (29%)
  starting transfers between devices  31.6 us (17%)
  local copies, waits for them, and re-layouts  16.7 us (9%)
  other arithmetic  6.96 us (4%)
    pallas_call x1, Pallas kernels, bwd(): pl.pallas_call(bwd_kernel, in_specs=[SMEM] + [VMEM] * 9, out_specs=[VMEM]...  33.4 us
    all_to_all x1, waiting for transfers between devices, on_device(): qd = lax.all_to_all(qd, PLANE, 0, 0, tiled=True).reshape(4, QT, 16, 1024)  27.4 us
    pallas_call x1, Pallas kernels, fwd(): pl.pallas_call(fwd_kernel, in_specs=[SMEM, VMEM, VMEM, VMEM, VMEM], out_s...  21.5 us
    all_to_all x1, waiting for transfers between devices, on_device(): own = lax.all_to_all(kv, PLANE, 0, 0, tiled=True)  17.5 us
    all_to_all x1, waiting for transfers between devices, on_device(): lax.all_to_all(oq.reshape(64, 16, 1024), PLANE, 0, 0, tiled=True)  17 us
    all_to_all x1, starting transfers between devices, on_device(): own = lax.all_to_all(kv, PLANE, 0, 0, tiled=True)  11.5 us
    all_to_all x1, starting transfers between devices, on_device(): lax.all_to_all(oq.reshape(64, 16, 1024), PLANE, 0, 0, tiled=True)  6.57 us
    all_to_all x1, starting transfers between devices, on_device(): lax.all_to_all(dkv, PLANE, 0, 0, tiled=True).reshape(4, 8, 2, 32, 2, HD)  5.72 us
  transfers between devices with their start and end apart: 9, of which 8 were waited for; matrix products, arithmetic and copies ran while one was open for 7% of the time, Pallas kernels for 0%

commit v1 on v0

v1 whole, which is shorter than its diff:
```python
import jax
import jax.numpy as jnp
from jax import lax
from jax.experimental import pallas as pl
from jax.experimental.pallas import tpu as pltpu
from jax.sharding import Mesh
from jax.sharding import PartitionSpec as P

HD = 128
NEG = -1.0e30
SCALE = HD ** -0.5
SC2 = SCALE * 1.4426950408889634
QT = 16
KP = 16
LIST = 160
WIDE = 1536
bf16, f32, i32 = jnp.bfloat16, jnp.float32, jnp.int32
VMEM = pl.BlockSpec(memory_space=pltpu.VMEM)
SMEM = pl.BlockSpec(memory_space=pltpu.SMEM)


def nt(a, b):
    return lax.dot_general(a, b, (((1,), (1,)), ((), ())), preferred_element_type=f32)


def nn(a, b):
    return jnp.dot(a, b, preferred_element_type=f32)


def row_tile(ref, n, first):
    n = jnp.minimum(n, QT - 1)
    return jnp.concatenate([ref[:, n, :, first + h * HD:first + (h + 1) * HD].reshape(64, HD) for h in range(4)], axis=0)


def key_tile(own_ref, oth_ref, p, first):
    parts = [own_ref[:, p, :, 1024 + 256 * h + first:1024 + 256 * h + first + HD].reshape(64, HD) for h in (0, 1)]
    parts += [oth_ref[:, p, :, 256 * h + first:256 * h + first + HD].reshape(64, HD) for h in (0, 1)]
    return jnp.concatenate(parts, axis=0)


def unpack(steps, kind, t):
    word = steps[kind, t]
    return lax.shift_right_logical(word, 8), word & 255


def mask_scores(s, n, p, pos_ref, kpos_ref, low):
    kpos = kpos_ref[...]
    kpos = jnp.concatenate([kpos, kpos], axis=1)
    first = p * 1024
    seen = (kpos <= pos_ref[n, 0:1, :] - first) & (kpos >= pos_ref[n, 1:2, :] - first)
    return jnp.where(seen, s, low)


def lanes_at(ref, p):
    return ref[:, pl.ds(pl.multiple_of(p * 256, 256), 256)]


def walk(count, score, soften, gather):
    score(0, 0)
    score(1, 1)
    trips = lax.shift_right_logical(count + 3, 2)

    @pl.loop(0, trips)
    def _(i):
        t = 4 * i
        for half in (0, 2):
            cur, nxt = half, 2 - half
            for k in (0, 1):
                score(t + half + 2 + k, nxt + k)
            for k in (0, 1):
                gather(jnp.maximum(t + half - 2 + k, 0), nxt + k)
            for k in (0, 1):
                soften(t + half + k, cur + k)

    last = jnp.maximum(4 * trips - 2, 0)
    gather(last, 2)
    gather(last + 1, 3)


def fwd_kernel(steps, pos_ref, kpos_ref, own_ref, oth_ref, ot_ref, st_ref, vt, m_s, l_s, acc, s_buf, p_buf, a_buf):
    @pl.loop(0, KP, unroll=4)
    def _(p):
        vt[:, pl.ds(pl.multiple_of(p * 256, 256), 256)] = key_tile(own_ref, oth_ref, p, HD).T

    m_s[...] = jnp.full_like(m_s, NEG)
    l_s[...] = jnp.zeros_like(l_s)
    acc[...] = jnp.zeros_like(acc)

    def run(kind):
        def score(t, buf):
            n, p = unpack(steps, kind, t)
            s = nt(key_tile(own_ref, oth_ref, p, 0), row_tile(own_ref, n, 0)) * SC2
            s_buf[buf] = mask_scores(s, n, p, pos_ref, kpos_ref, 2 * NEG) if kind else s

        def soften(t, buf):
            n, _ = unpack(steps, kind, t)
            s = s_buf[buf]
            old = m_s[n]
            new = jnp.maximum(old, jnp.max(s, axis=0, keepdims=True))
            w = jnp.exp2(s - new)
            alpha = jnp.exp2(old - new)
            m_s[n] = new
            l_s[n] = l_s[n] * alpha + jnp.sum(w, axis=0, keepdims=True)
            a_buf[buf] = alpha
            p_buf[buf] = w.astype(bf16)

        def gather(t, buf):
            n, p = unpack(steps, kind, t)
            acc[n] = acc[n] * a_buf[buf] + nn(lanes_at(vt, p), p_buf[buf])

        for buf in (2, 3):
            p_buf[buf] = jnp.zeros((256, 256), bf16)
            a_buf[buf] = jnp.ones((1, 256), f32)
        walk(steps[kind, LIST - 1], score, soften, gather)

    run(0)
    run(1)

    @pl.loop(0, QT, unroll=4)
    def _(n):
        o = acc[n]
        ot_ref[n] = o
        st_ref[n, 0:1, :] = m_s[n]
        st_ref[n, 1:2, :] = l_s[n]
        st_ref[n, 2:3, :] = jnp.sum(row_tile(own_ref, n, 512).T.astype(f32) * o, axis=0, keepdims=True)


def bwd_kernel(steps, pos_ref, kpos_ref, st0_ref, st1_ref, st2_ref, st3_ref, own_ref, oth_ref, ot_ref,
               out_ref, oth_out_ref, kt, lse_s, delta_s, w_s, dq, dk, dv, s_buf, dp_buf, p_buf, ds_buf):
    @pl.loop(0, KP, unroll=4)
    def _(p):
        kt[:, pl.ds(pl.multiple_of(p * 256, 256), 256)] = key_tile(own_ref, oth_ref, p, 0).T

    refs = (st0_ref, st1_ref, st2_ref, st3_ref)

    @pl.loop(0, QT, unroll=4)
    def _(n):
        top = refs[0][n, 0:1, :]
        for ref in refs[1:]:
            top = jnp.maximum(top, ref[n, 0:1, :])
        share = [jnp.exp2(ref[n, 0:1, :] - top) for ref in refs]
        total = sum(w * ref[n, 1:2, :] for w, ref in zip(share, refs))
        lse_s[n] = top + jnp.log2(total)
        delta_s[n] = sum(w * ref[n, 2:3, :] for w, ref in zip(share, refs)) / total
        w_s[n] = share[0] / total
    lse_s[QT] = jnp.full((1, 256), -NEG, f32)
    delta_s[QT] = jnp.zeros((1, 256), f32)
    dq[...] = jnp.zeros_like(dq)
    dk[...] = jnp.zeros_like(dk)
    dv[...] = jnp.zeros_like(dv)

    def run(kind):
        def score(t, buf):
            n, p = unpack(steps, kind, t)
            s = nt(key_tile(own_ref, oth_ref, p, 0), row_tile(own_ref, n, 0)) * SC2
            s_buf[buf] = mask_scores(s, n, p, pos_ref, kpos_ref, NEG) if kind else s
            dp_buf[buf] = nt(key_tile(own_ref, oth_ref, p, HD), row_tile(own_ref, n, 512))

        def soften(t, buf):
            n, _ = unpack(steps, kind, t)
            w = jnp.exp2(s_buf[buf] - lse_s[n])
            p_buf[buf] = w.astype(bf16)
            ds_buf[buf] = (w * (dp_buf[buf] - delta_s[n])).astype(bf16)

        def gather(t, buf):
            n, p = unpack(steps, kind, t)
            ds = ds_buf[buf]
            dv[p] += nn(p_buf[buf], row_tile(own_ref, n, 512))
            dk[p] += nn(ds, row_tile(own_ref, n, 0))
            dq[n] += nn(lanes_at(kt, p), ds)

        for buf in (2, 3):
            p_buf[buf] = jnp.zeros((256, 256), bf16)
            ds_buf[buf] = jnp.zeros((256, 256), bf16)
        walk(steps[kind, LIST - 1], score, soften, gather)

    run(0)
    run(1)

    @pl.loop(0, QT, unroll=4)
    def _(n):
        ob = (ot_ref[n] * w_s[n]).astype(bf16).T
        qb = (dq[n] * SCALE).astype(bf16).T
        for h in range(4):
            out_ref[:, n, :, h * HD:(h + 1) * HD] = ob[h * 64:(h + 1) * 64].reshape(4, 16, HD)
            out_ref[:, n, :, 512 + h * HD:512 + (h + 1) * HD] = qb[h * 64:(h + 1) * 64].reshape(4, 16, HD)

    @pl.loop(0, KP, unroll=4)
    def _(p):
        for first, tile in ((0, (dk[p] * SCALE).astype(bf16)), (HD, dv[p].astype(bf16))):
            for h in (0, 1):
                at = 256 * h + first
                out_ref[:, p, :, 1024 + at:1024 + at + HD] = tile[64 * h:64 * h + 64].reshape(4, 16, HD)
                oth_out_ref[:, p, :, at:at + HD] = tile[128 + 64 * h:192 + 64 * h].reshape(4, 16, HD)


def fwd(steps, pos, kpos, own, oth):
    return pl.pallas_call(
        fwd_kernel,
        in_specs=[SMEM] + [VMEM] * 4,
        out_specs=[VMEM, VMEM],
        scratch_shapes=[
            pltpu.VMEM((HD, KP * 256), bf16),
            pltpu.VMEM((QT + 1, 1, 256), f32), pltpu.VMEM((QT + 1, 1, 256), f32), pltpu.VMEM((QT + 1, HD, 256), f32),
            pltpu.VMEM((4, 256, 256), f32), pltpu.VMEM((4, 256, 256), bf16), pltpu.VMEM((4, 1, 256), f32),
        ],
        out_shape=[jax.ShapeDtypeStruct((QT, HD, 256), f32), jax.ShapeDtypeStruct((QT, 4, 256), f32)],
        compiler_params=pltpu.CompilerParams(vmem_limit_bytes=40 << 20),
        name="fwd",
    )(steps, pos, kpos, own, oth)


def bwd(steps, pos, kpos, sts, own, oth, ot):
    return pl.pallas_call(
        bwd_kernel,
        in_specs=[SMEM] + [VMEM] * 9,
        out_specs=[VMEM] * 2,
        scratch_shapes=[
            pltpu.VMEM((HD, KP * 256), bf16),
            pltpu.VMEM((QT + 1, 1, 256), f32), pltpu.VMEM((QT + 1, 1, 256), f32), pltpu.VMEM((QT + 1, 1, 256), f32),
            pltpu.VMEM((QT + 1, HD, 256), f32), pltpu.VMEM((KP, 256, HD), f32), pltpu.VMEM((KP, 256, HD), f32),
            pltpu.VMEM((4, 256, 256), f32), pltpu.VMEM((4, 256, 256), f32),
            pltpu.VMEM((4, 256, 256), bf16), pltpu.VMEM((4, 256, 256), bf16),
        ],
        out_shape=[jax.ShapeDtypeStruct((4, QT, 16, WIDE), bf16), jax.ShapeDtypeStruct((4, KP, 16, 512), bf16)],
        compiler_params=pltpu.CompilerParams(vmem_limit_bytes=48 << 20),
        name="bwd",
    )(steps, pos, kpos, *sts, own, oth, ot)


def pack_kernel(q_ref, k_ref, v_ref, do_ref, out_ref):
    for j in range(4):
        for u in range(8):
            for g in range(2):
                at = j * 16 + u * 2 + g
                out_ref[at, :, 0:512] = q_ref[16 * u:16 * u + 16, 512 * g:512 * g + 512]
                out_ref[at, :, 512:1024] = do_ref[16 * u:16 * u + 16, 512 * g:512 * g + 512]
                for h in (0, 1):
                    rows = slice(32 * j + 16 * h, 32 * j + 16 * h + 16)
                    out_ref[at, :, 1024 + 256 * h:1152 + 256 * h] = k_ref[rows, HD * g:HD * g + HD]
                    out_ref[at, :, 1152 + 256 * h:1280 + 256 * h] = v_ref[rows, HD * g:HD * g + HD]


def pack(q, k, v, do):
    return pl.pallas_call(
        pack_kernel, in_specs=[VMEM] * 4, out_specs=VMEM,
        out_shape=jax.ShapeDtypeStruct((64, 16, WIDE), bf16),
        compiler_params=pltpu.CompilerParams(vmem_limit_bytes=24 << 20), name="pack",
    )(q, k, v, do)


def add_kernel(own_ref, other_ref, out_ref):
    out_ref[...] = (own_ref[...].astype(f32) + other_ref[...].astype(f32)).astype(bf16)


def add_other(out, other):
    last = pl.BlockSpec((4, KP, 16, 512), lambda i: (0, 0, 0, 2))
    return pl.pallas_call(
        add_kernel, grid=(1,), in_specs=[last, pl.BlockSpec((4, KP, 16, 512), lambda i: (0, 0, 0, 0))], out_specs=last,
        out_shape=jax.ShapeDtypeStruct(out.shape, bf16), input_output_aliases={0: 0},
        compiler_params=pltpu.CompilerParams(vmem_limit_bytes=24 << 20), name="add_cores",
    )(out, other)


def sum_kernel(in_ref, at_ref, qg_ref, kg_ref, vg_ref):
    for u in range(8):
        for g in range(2):
            rows, cols = slice(16 * u, 16 * u + 16), slice(512 * g, 512 * g + 512)
            for first, ref in ((0, at_ref), (512, qg_ref)):
                parts = [in_ref[j * 16 + u * 2 + g, :, first:first + 512].astype(f32) for j in range(4)]
                ref[rows, cols] = (parts[0] + parts[1] + parts[2] + parts[3]).astype(bf16)
    for j in range(4):
        for g in range(2):
            for h in (0, 1):
                rows, cols = slice(32 * j + 16 * h, 32 * j + 16 * h + 16), slice(HD * g, HD * g + HD)
                both = sum(in_ref[j * 16 + u * 2 + g, :, 1024 + 256 * h:1280 + 256 * h].astype(f32) for u in range(8))
                kg_ref[rows, cols] = both[:, :HD].astype(bf16)
                vg_ref[rows, cols] = both[:, HD:].astype(bf16)


def sum_pieces(pieces):
    big, small = jax.ShapeDtypeStruct((128, 1024), bf16), jax.ShapeDtypeStruct((128, 256), bf16)
    return pl.pallas_call(
        sum_kernel, in_specs=[VMEM], out_specs=[VMEM] * 4, out_shape=[big, big, small, small],
        compiler_params=pltpu.CompilerParams(vmem_limit_bytes=24 << 20), name="sum_pieces",
    )(pieces)


def make_plan(lengths, core, u, j):
    n = jnp.arange(QT + 1, dtype=i32)[:, None, None]
    x = jnp.arange(4, dtype=i32)[None, :, None]
    t = jnp.arange(16, dtype=i32)[None, None, :]
    pos = (512 * (2 * n + core) + 128 * x + 16 * u + t).reshape(QT + 1, 64)
    ends = jnp.cumsum(lengths)
    start = jnp.sum(jnp.where(ends[None, None, :] <= pos[:, :, None], lengths, 0), axis=-1)
    rows = jnp.stack([jnp.tile(pos, (1, 4)), jnp.tile(start, (1, 4))], axis=1).astype(i32)
    low = (start[:QT, 0] // 1024)[None, :]
    plain_low = ((start[:QT, -1] + 1023) // 1024)[None, :]
    d = jnp.arange(KP, dtype=i32)[:, None]
    m = jnp.arange(QT, dtype=i32)[None, :]
    live = (m - d >= 0) & (m - d >= low)
    plain = live & (d > 0) & (m - d >= plain_low)
    code = (m * 256 + m - d).reshape(1, QT * KP)
    at = jnp.arange(LIST, dtype=i32)[:, None]

    def compact(mask):
        mask = mask.reshape(1, QT * KP)
        rank = jnp.cumsum(mask.astype(i32), axis=1) - 1
        listed = QT * 256 + jnp.sum(jnp.where(mask & (rank == at), code - QT * 256, 0), axis=1)
        return jnp.where(at[:, 0] == LIST - 1, rank[0, -1] + 1, listed)

    steps = jnp.stack([compact(plain), compact(live & ~plain)]).astype(i32)
    r = jnp.arange(256, dtype=i32)
    parity = jnp.where(r < 128, core, 1 - core)
    kpos = 512 * parity + 128 * (r % 64 // 16) + 32 * j + 16 * (r // 64 % 2) + r % 16
    return steps, rows, jnp.broadcast_to(kpos[:, None], (256, 128)).astype(i32)


PLANE = ("head", "inner", "zl")


def on_device(query_rows, key_rows, value_rows, out_grad, lengths):
    j, u, core = (lax.axis_index(name) for name in ("head", "inner", "core"))
    swap = [(0, 1), (1, 0)]
    steps, pos, kpos = make_plan(lengths, core, u, j)
    pieces = pack(query_rows.reshape(128, 1024), key_rows.reshape(128, 256), value_rows.reshape(128, 256),
                  out_grad.reshape(128, 1024))
    own = lax.all_to_all(pieces, PLANE, 0, 0, tiled=True).reshape(4, QT, 16, WIDE)
    oth = lax.ppermute(own[..., 1024:], "core", swap)
    ot, st = fwd(steps, pos, kpos, own, oth)
    sts = [st] + [lax.ppermute(st, "head", [(i, (i + k) % 4) for i in range(4)]) for k in (1, 2, 3)]
    out, oth_out = bwd(steps, pos, kpos, sts, own, oth, ot)
    out = add_other(out, lax.ppermute(oth_out, "core", swap))
    out = lax.all_to_all(out.reshape(64, 16, WIDE), PLANE, 0, 0, tiled=True)
    attended, query_grad, key_grad, value_grad = sum_pieces(out)
    return (attended.reshape(1, 1, 128, 1024), query_grad.reshape(1, 1, 128, 1024),
            key_grad.reshape(1, 1, 128, 256), value_grad.reshape(1, 1, 128, 256))


def solution(mesh):
    finer = Mesh(mesh.devices.reshape(4, 8, 2, 2), ("head", "inner", "zl", "core"))
    placed = P(("inner", "zl", "core"), "head", None, None)
    return jax.shard_map(
        on_device,
        mesh=finer,
        in_specs=(placed, placed, placed, placed, P()),
        out_specs=(placed, placed, placed, placed),
        check_vma=False,
    )
```

time: 187 us -> 173 us (0.925)
  blocking collectives: 0 us -> 48 us
  waiting for transfers between devices: 75 us -> 44.7 us
  starting transfers between devices: 31.6 us -> 14.8 us
  Pallas kernels: 54.9 us -> 46.2 us
  other arithmetic: 6.96 us -> 2 us
  local copies, waits for them, and re-layouts: 16.7 us -> 12.8 us
  between operations: 0.93 us -> 3.49 us
    all_to_all x0 -> x1, blocking collectives: none -> 48 us  [on_device(): out = lax.all_to_all(out.reshape(64, 16, WIDE), PLANE, 0, 0, tiled=True)]
    all_to_all x4 -> x1, waiting for transfers between devices: 67.4 us -> 36.8 us  [on_device(): lax.all_to_all(pieces, PLANE, 0, 0, tiled=True).reshape(4, QT, 16, WIDE)]
    all_to_all x4 -> x1, starting transfers between devices: 28.6 us -> 11.6 us  [on_device(): lax.all_to_all(pieces, PLANE, 0, 0, tiled=True).reshape(4, QT, 16, WIDE)]
    reshape x6 -> x0, local copies, waits for them, and re-layouts: 6.77 us -> none  [the longest x1 3.31 us: on_device(): lax.all_to_all(oq.reshape(64, 16, 1024), PLANE, 0, 0, tiled=True)]
    unnamed x10 -> x16, local copies, waits for them, and re-layouts: 1.33 us -> 7.13 us
    pallas_call x1, Pallas kernels: 33.4 us -> 28.1 us  [bwd(): pl.pallas_call(bwd_kernel, in_specs=[SMEM] + [VMEM] * 9, out_specs=[VMEM]...]
    reduce_sum x2 -> x1, other arithmetic: 4.35 us -> 0.16 us  [compact(): jnp.sum(jnp.where(mask & (rank == at), code - QT * 256, 0), axis=1)]
    pallas_call x1 -> x4, Pallas kernels: 21.5 us -> 18.1 us  [the longest x1 15.9 us: fwd(): pl.pallas_call(fwd_kernel, in_specs=[SMEM] + [VMEM] * 4, out_specs=[VMEM,...]
  transfers between devices with their start and end apart: 9 -> 6, of which waited for: 8 -> 5; matrix products, arithmetic and copies ran while one was open for 7% -> 4% of each run, Pallas kernels for 0% -> 0%
where the time goes in v1:
time: 173 us; the launch traced here: 172 us
  blocking collectives  48 us (28%)
  Pallas kernels  46.2 us (27%)
  waiting for transfers between devices  44.7 us (26%)
  starting transfers between devices  14.8 us (9%)
  local copies, waits for them, and re-layouts  12.8 us (7%)
  between operations  3.49 us (2%)
  other arithmetic  2 us (1%)
    all_to_all x1, blocking collectives, on_device(): out = lax.all_to_all(out.reshape(64, 16, WIDE), PLANE, 0, 0, tiled=True)  48 us
    all_to_all x1, waiting for transfers between devices, on_device(): lax.all_to_all(pieces, PLANE, 0, 0, tiled=True).reshape(4, QT, 16, WIDE)  36.8 us
    pallas_call x1, Pallas kernels, bwd(): pl.pallas_call(bwd_kernel, in_specs=[SMEM] + [VMEM] * 9, out_specs=[VMEM]...  28.1 us
    pallas_call x1, Pallas kernels, fwd(): pl.pallas_call(fwd_kernel, in_specs=[SMEM] + [VMEM] * 4, out_specs=[VMEM,...  15.9 us
    all_to_all x1, starting transfers between devices, on_device(): lax.all_to_all(pieces, PLANE, 0, 0, tiled=True).reshape(4, QT, 16, WIDE)  11.6 us
    unnamed x16, local copies, waits for them, and re-layouts  7.13 us
    ppermute x3, waiting for transfers between devices, on_device(): lax.ppermute(st, 'head', [(i, (i + k) % 4) for i in range(4)])  5.19 us
  transfers between devices with their start and end apart: 6, of which 5 were waited for; matrix products, arithmetic and copies ran while one was open for 4% of the time, Pallas kernels for 0%

profile of v1, /device:TPU:0, one launch (start us, length us, event | category | flops | bytes accessed | tf_op | source)
XLA Modules:
  0.0 172.0 jit_solution(368105012987860667)
XLA Ops:
  0.6 0.0 copy-start.3
  0.6 0.9 copy-done.3
  1.6 0.9 copy-done.4
  2.5 0.8 copy-done.5
  3.4 0.8 copy-done.6
  4.2 0.3 pack.1
  4.5 1.7 copy-done.2
  6.2 11.6 %all-to-all-start = ((bf16[64,16,1536]{2,1,0:T(8,128)(2,1)}), bf16[64,16,1536]{2,1,0:T(8,128)(2,1)S(1)}, u32[]{:S(2)}, u32[]{:S(2)}) async-start(bf16[64,16,1536]{2,1,0:T(8,128)(2,1)} %copy-done.2), calls=%async_computation | async-start | bytes 6291456 | tf_op jit(solution)/shard_map/all_to_all | solution.py:328
  17.9 0.1 and.225
  18.0 0.1 and.226
  18.1 0.1 and.218
  18.1 0.1 and.219
  18.2 0.1 add.245
  18.3 0.1 sub.182
  18.4 0.1 sub.187
  18.5 0.1 sub.188
  18.6 0.1 sub.201
  18.6 0.1 add_add_fusion
  18.7 0.1 add.242
  18.8 0.1 add.243
  18.9 0.0 copy-done.7
  18.9 0.2 reduce-window.21
  19.1 0.1 select_reduce_fusion.2
  19.2 0.2 slice_reduce_fusion
  19.4 0.1 ge.131
  19.5 0.1 and.224
  19.6 0.1 ge.118
  19.7 0.1 ge.122
  19.8 0.3 reduce-window.31
  20.1 0.2 slice_reduce_fusion.1
  20.3 0.2 reduce-window.32
  20.5 0.3 reduce-window.24
  20.8 0.2 slice_reduce_fusion.2
  21.0 0.2 reduce-window.30
  21.1 0.1 fusion.14
  21.2 0.1 fusion.15
  21.3 0.2 select_reduce_fusion.1
  21.5 36.8 %all-to-all-done = bf16[64,16,1536]{2,1,0:T(8,128)(2,1)S(1)} async-done(((bf16[64,16,1536]{2,1,0:T(8,128)(2,1)}), bf16[64,16,1536]{2,1,0:T(8,128)(2,1)S(1)}, u32[]{:S(2)}, u32[]{:S(2)}) %all-to-all-start) | async-done | bytes 3145760 | tf_op jit(solution)/shard_map/all_to_all | solution.py:328
  58.3 1.1 slice.42
  59.4 0.0 collective-permute-start
  59.4 0.8 slice.40
  60.2 0.1 broadcast.617
  60.2 0.6 slice.41
  60.8 0.6 slice.38
  61.4 0.1 broadcast.611
  61.5 0.6 slice.39
  64.7 0.1 tile.18
  64.8 0.1 tile.16
  65.0 0.0 collective-permute-done.oth_ref
  65.0 0.1 broadcast_in_dim.64.kpos_ref
  65.1 15.9 %fwd.1 = (f32[16,128,256]{2,1,0:T(8,128)S(1)}, f32[16,4,256]{2,1,0:T(4,128)S(1)}) custom-call(s32[2,160]{1,0:T(2,128)S(1)} %pad_add_fusion.1.steps, s32[17,2,256]{2,1,0:T(2,128)S(1)} %pad_add_fusion.pos_ref, s32[256,128]{1,0:T(8,128)S(1)} %broadcast_in_dim.64.kpos_ref, bf16[4,16,16,1536]{3,2,1,0:T(8,128)(2,1)S(1)} %bitcast.40, ...), custom_call_target="tpu_custom_call" | custom-call | tf_op jit(solution)/shard_map/fwd/pallas_call | solution.py:198
  81.0 1.3 collective-permute-start.3
  82.3 1.4 collective-permute-start.2
  83.7 0.5 collective-permute-start.1
  84.2 1.8 %collective-permute-done.3.st3_ref = f32[16,4,256]{2,1,0:T(4,128)S(1)} collective-permute-done((f32[16,4,256]{2,1,0:T(4,128)S(1)}, f32[16,4,256]{2,1,0:T(4,128)S(1)}, u32[]{:S(2)}, u32[]{:S(2)}) %collective-permute-start.3) | collective-permute-done | bytes 65568 | tf_op jit(solution)/shard_map/ppermute | solution.py:331
  86.0 2.6 %collective-permute-done.2.st2_ref = f32[16,4,256]{2,1,0:T(4,128)S(1)} collective-permute-done((f32[16,4,256]{2,1,0:T(4,128)S(1)}, f32[16,4,256]{2,1,0:T(4,128)S(1)}, u32[]{:S(2)}, u32[]{:S(2)}) %collective-permute-start.2) | collective-permute-done | bytes 65568 | tf_op jit(solution)/shard_map/ppermute | solution.py:331
  88.6 0.8 collective-permute-done.1.st1_ref
  89.4 28.1 %bwd.1 = (bf16[4,16,16,1536]{3,2,1,0:T(8,128)(2,1)}, bf16[4,16,16,512]{3,2,1,0:T(8,128)(2,1)S(1)}) custom-call(s32[2,160]{1,0:T(2,128)S(1)} %pad_add_fusion.1.steps, s32[17,2,256]{2,1,0:T(2,128)S(1)} %pad_add_fusion.pos_ref, s32[256,128]{1,0:T(8,128)S(1)} %broadcast_in_dim.64.kpos_ref, f32[16,4,256]{2,1,0:T(4,128)S(1)} %get-tuple-element.12.st0_ref, ...), custom_call_target="tpu_custom_call" | custom-call | tf_op jit(solution)/shard_map/bwd/pallas_call | solution.py:214
  117.5 0.0 collective-permute-start.4
  117.5 2.7 %collective-permute-done.4.other_ref = bf16[4,16,16,512]{3,2,1,0:T(8,128)(2,1)S(1)} collective-permute-done((bf16[4,16,16,512]{3,2,1,0:T(8,128)(2,1)S(1)}, bf16[4,16,16,512]{3,2,1,0:T(8,128)(2,1)S(1)}, u32[]{:S(2)}, u32[]{:S(2)}) %collective-permute-start.4) | collective-permute-done | bytes 1048608 | tf_op jit(solution)/shard_map/ppermute | solution.py:333
  120.2 1.9 %copy-done.1 = bf16[4,16,16,1536]{3,2,1,0:T(8,128)(2,1)S(1)} copy-done((bf16[4,16,16,1536]{3,2,1,0:T(8,128)(2,1)S(1)}, bf16[4,16,16,1536]{3,2,1,0:T(8,128)(2,1)}, u32[]{:S(2)}) %copy-start.1) | copy-done | bytes 3145752
  122.1 0.8 add_cores.1
  122.9 48.0 %all_to_all.10.in_ref = bf16[64,16,1536]{2,1,0:T(8,128)(2,1)S(1)} all-to-all(bf16[64,16,1536]{2,1,0:T(8,128)(2,1)S(1)} %bitcast.42), channel_id=1, replica_groups=mesh['head'=4,'inner'=8,'zl'=2,'core'=2] {'head','inner','zl'}, dimensions={0} | all-to-all | bytes 6291456 | tf_op jit(solution)/shard_map/all_to_all | solution.py:334
  170.9 1.1 sum_pieces.1
  (37 shorter events, 0.2 us)
Async XLA Ops:
  0.6 1.0 copy-start.3
  1.6 0.9 copy-start.4
  2.5 0.8 copy-start.5
  3.4 0.8 copy-start.6
  4.5 1.7 copy-start.2
  6.2 12.7 %copy-start.7 = (s32[4]{0:T(128)S(1)}, s32[4]{0:T(128)}, u32[]{:S(2)}) copy-start(s32[4]{0:T(128)} %param.9) | copy-start | bytes 52
  6.2 52.1 %all-to-all-start = ((bf16[64,16,1536]{2,1,0:T(8,128)(2,1)}), bf16[64,16,1536]{2,1,0:T(8,128)(2,1)S(1)}, u32[]{:S(2)}, u32[]{:S(2)}) async-start(bf16[64,16,1536]{2,1,0:T(8,128)(2,1)} %copy-done.2), calls=%async_computation | async-start | bytes 6291456 | tf_op jit(solution)/shard_map/all_to_all | solution.py:328
  58.3 22.8 %copy-start = (bf16[64,16,1536]{2,1,0:T(8,128)(2,1)}, bf16[64,16,1536]{2,1,0:T(8,128)(2,1)S(1)}, u32[]{:S(2)}) copy-start(bf16[64,16,1536]{2,1,0:T(8,128)(2,1)S(1)} %all-to-all-done) | copy-start | bytes 9437188
  59.4 5.6 %collective-permute-start = (bf16[4,16,16,512]{3,2,1,0:T(8,128)(2,1)}, bf16[4,16,16,512]{3,2,1,0:T(8,128)(2,1)}, u32[]{:S(2)}, u32[]{:S(2)}) collective-permute-start(bf16[4,16,16,512]{3,2,1,0:T(8,128)(2,1)} %slice.42), channel_id=1, source_target_pairs={{0,1},{1,0},{2,3},{3,2},{4,5},{5,4},{6,7},{7,6},{8,9},{9,8},{10,11... | collective-permute-start | bytes 3145736 | tf_op jit(solution)/shard_map/ppermute | solution.py:329
  81.0 5.0 %collective-permute-start.3 = (f32[16,4,256]{2,1,0:T(4,128)S(1)}, f32[16,4,256]{2,1,0:T(4,128)S(1)}, u32[]{:S(2)}, u32[]{:S(2)}) collective-permute-start(f32[16,4,256]{2,1,0:T(4,128)S(1)} %get-tuple-element.12.st0_ref), channel_id=1, source_target_pairs={{0,96},{32,0},{64,32},{96,64},{1,97},{33,1},{65,33},{97,65},{2,98}... | collective-permute-start | bytes 196616 | tf_op jit(solution)/shard_map/ppermute | solution.py:331
  82.3 6.3 %collective-permute-start.2 = (f32[16,4,256]{2,1,0:T(4,128)S(1)}, f32[16,4,256]{2,1,0:T(4,128)S(1)}, u32[]{:S(2)}, u32[]{:S(2)}) collective-permute-start(f32[16,4,256]{2,1,0:T(4,128)S(1)} %get-tuple-element.12.st0_ref), channel_id=1, source_target_pairs={{0,64},{32,96},{64,0},{96,32},{1,65},{33,97},{65,1},{97,33},{2,66}... | collective-permute-start | bytes 196616 | tf_op jit(solution)/shard_map/ppermute | solution.py:331
  83.7 5.7 %collective-permute-start.1 = (f32[16,4,256]{2,1,0:T(4,128)S(1)}, f32[16,4,256]{2,1,0:T(4,128)S(1)}, u32[]{:S(2)}, u32[]{:S(2)}) collective-permute-start(f32[16,4,256]{2,1,0:T(4,128)S(1)} %get-tuple-element.12.st0_ref), channel_id=1, source_target_pairs={{0,32},{32,64},{64,96},{96,0},{1,33},{33,65},{65,97},{97,1},{2,34}... | collective-permute-start | bytes 196616 | tf_op jit(solution)/shard_map/ppermute | solution.py:331
  117.5 2.7 %collective-permute-start.4 = (bf16[4,16,16,512]{3,2,1,0:T(8,128)(2,1)S(1)}, bf16[4,16,16,512]{3,2,1,0:T(8,128)(2,1)S(1)}, u32[]{:S(2)}, u32[]{:S(2)}) collective-permute-start(bf16[4,16,16,512]{3,2,1,0:T(8,128)(2,1)S(1)} %get-tuple-element.15), channel_id=1, source_target_pairs={{0,1},{1,0},{2,3},{3,2},{4,5},{5,4},{6,7},{7,6},{8,9},{9,8},{10,11... | collective-permute-start | bytes 3145736 | tf_op jit(solution)/shard_map/ppermute | solution.py:333
  120.2 1.9 %copy-start.1 = (bf16[4,16,16,1536]{3,2,1,0:T(8,128)(2,1)S(1)}, bf16[4,16,16,1536]{3,2,1,0:T(8,128)(2,1)}, u32[]{:S(2)}) copy-start(bf16[4,16,16,1536]{3,2,1,0:T(8,128)(2,1)} %get-tuple-element.14.own_ref) | copy-start | bytes 9437188

commit v2 on v1

--- a/solution.py
+++ b/solution.py
@@ -67,10 +67,8 @@
             cur, nxt = half, 2 - half
             for k in (0, 1):
                 score(t + half + 2 + k, nxt + k)
-            for k in (0, 1):
+                soften(t + half + k, cur + k)
                 gather(jnp.maximum(t + half - 2 + k, 0), nxt + k)
-            for k in (0, 1):
-                soften(t + half + k, cur + k)
 
     last = jnp.maximum(4 * trips - 2, 0)
     gather(last, 2)
@@ -205,7 +203,7 @@
             pltpu.VMEM((4, 256, 256), f32), pltpu.VMEM((4, 256, 256), bf16), pltpu.VMEM((4, 1, 256), f32),
         ],
         out_shape=[jax.ShapeDtypeStruct((QT, HD, 256), f32), jax.ShapeDtypeStruct((QT, 4, 256), f32)],
-        compiler_params=pltpu.CompilerParams(vmem_limit_bytes=40 << 20),
+        compiler_params=pltpu.CompilerParams(vmem_limit_bytes=16 << 20),
         name="fwd",
     )(steps, pos, kpos, own, oth)
 
@@ -223,7 +221,7 @@
             pltpu.VMEM((4, 256, 256), bf16), pltpu.VMEM((4, 256, 256), bf16),
         ],
         out_shape=[jax.ShapeDtypeStruct((4, QT, 16, WIDE), bf16), jax.ShapeDtypeStruct((4, KP, 16, 512), bf16)],
-        compiler_params=pltpu.CompilerParams(vmem_limit_bytes=48 << 20),
+        compiler_params=pltpu.CompilerParams(vmem_limit_bytes=24 << 20),
         name="bwd",
     )(steps, pos, kpos, *sts, own, oth, ot)
 
@@ -245,7 +243,7 @@
     return pl.pallas_call(
         pack_kernel, in_specs=[VMEM] * 4, out_specs=VMEM,
         out_shape=jax.ShapeDtypeStruct((64, 16, WIDE), bf16),
-        compiler_params=pltpu.CompilerParams(vmem_limit_bytes=24 << 20), name="pack",
+        compiler_params=pltpu.CompilerParams(vmem_limit_bytes=12 << 20), name="pack",
     )(q, k, v, do)
 
 
@@ -258,7 +256,7 @@
     return pl.pallas_call(
         add_kernel, grid=(1,), in_specs=[last, pl.BlockSpec((4, KP, 16, 512), lambda i: (0, 0, 0, 0))], out_specs=last,
         out_shape=jax.ShapeDtypeStruct(out.shape, bf16), input_output_aliases={0: 0},
-        compiler_params=pltpu.CompilerParams(vmem_limit_bytes=24 << 20), name="add_cores",
+        compiler_params=pltpu.CompilerParams(vmem_limit_bytes=12 << 20), name="add_cores",
     )(out, other)
 
 
@@ -282,7 +280,7 @@
     big, small = jax.ShapeDtypeStruct((128, 1024), bf16), jax.ShapeDtypeStruct((128, 256), bf16)
     return pl.pallas_call(
         sum_kernel, in_specs=[VMEM], out_specs=[VMEM] * 4, out_shape=[big, big, small, small],
-        compiler_params=pltpu.CompilerParams(vmem_limit_bytes=24 << 20), name="sum_pieces",
+        compiler_params=pltpu.CompilerParams(vmem_limit_bytes=12 << 20), name="sum_pieces",
     )(pieces)
 
 
@@ -291,7 +289,8 @@
     x = jnp.arange(4, dtype=i32)[None, :, None]
     t = jnp.arange(16, dtype=i32)[None, None, :]
     pos = (512 * (2 * n + core) + 128 * x + 16 * u + t).reshape(QT + 1, 64)
-    ends = jnp.cumsum(lengths)
+    docs = jnp.arange(lengths.shape[0])
+    ends = jnp.sum(jnp.where(docs[:, None] <= docs[None, :], lengths[:, None], 0), axis=0)
     start = jnp.sum(jnp.where(ends[None, None, :] <= pos[:, :, None], lengths, 0), axis=-1)
     rows = jnp.stack([jnp.tile(pos, (1, 4)), jnp.tile(start, (1, 4))], axis=1).astype(i32)
     low = (start[:QT, 0] // 1024)[None, :]
@@ -301,13 +300,15 @@
     live = (m - d >= 0) & (m - d >= low)
     plain = live & (d > 0) & (m - d >= plain_low)
     code = (m * 256 + m - d).reshape(1, QT * KP)
+    order = jnp.arange(QT * KP, dtype=i32)
+    earlier = order[:, None] < order[None, :]
     at = jnp.arange(LIST, dtype=i32)[:, None]
 
     def compact(mask):
         mask = mask.reshape(1, QT * KP)
-        rank = jnp.cumsum(mask.astype(i32), axis=1) - 1
+        rank = jnp.sum((earlier & mask.reshape(QT * KP, 1)).astype(i32), axis=0, keepdims=True)
         listed = QT * 256 + jnp.sum(jnp.where(mask & (rank == at), code - QT * 256, 0), axis=1)
-        return jnp.where(at[:, 0] == LIST - 1, rank[0, -1] + 1, listed)
+        return jnp.where(at[:, 0] == LIST - 1, jnp.sum(mask.astype(i32)), listed)
 
     steps = jnp.stack([compact(plain), compact(live & ~plain)]).astype(i32)
     r = jnp.arange(256, dtype=i32)

time: 173 us -> 161 us (0.931); the launches traced: 172 us -> 158 us
  Pallas kernels: 46.2 us -> 37.4 us
  local copies, waits for them, and re-layouts: 12.8 us -> 7.27 us
  between operations: 3.49 us -> 0.83 us
  waiting for transfers between devices: 44.7 us -> 47.3 us
    pallas_call x1, Pallas kernels: 28.1 us -> 22.4 us  [bwd(): pl.pallas_call(bwd_kernel, in_specs=[SMEM] + [VMEM] * 9, out_specs=[VMEM]...]
    pallas_call x1, Pallas kernels: 15.9 us -> 12.7 us  [fwd(): pl.pallas_call(fwd_kernel, in_specs=[SMEM] + [VMEM] * 4, out_specs=[VMEM,...]
    slice x5 -> x0, local copies, waits for them, and re-layouts: 2.71 us -> none  [the longest x4 2.52 us: compact(): return jnp.where(at[:, 0] == LIST - 1, rank[0, -1] + 1, listed)]
    all_to_all x1, waiting for transfers between devices: 36.8 us -> 38.8 us  [on_device(): lax.all_to_all(pieces, PLANE, 0, 0, tiled=True).reshape(4, QT, 16, WIDE)]
    unnamed x16 -> x12, local copies, waits for them, and re-layouts: 7.13 us -> 5.24 us
  transfers between devices with their start and end apart: 6 -> 6, of which waited for: 5 -> 6; matrix products, arithmetic and copies ran while one was open for 4% -> 2% of each run, Pallas kernels for 0% -> 0%
where the time goes in v2:
time: 161 us; the launch traced here: 158 us
  blocking collectives  47.7 us (30%)
  waiting for transfers between devices  47.3 us (29%)
  Pallas kernels  37.4 us (23%)
  starting transfers between devices  14.8 us (9%)
  local copies, waits for them, and re-layouts  7.27 us (5%)
  other arithmetic  2.99 us (2%)
    all_to_all x1, blocking collectives, on_device(): out = lax.all_to_all(out.reshape(64, 16, WIDE), PLANE, 0, 0, tiled=True)  47.7 us
    all_to_all x1, waiting for transfers between devices, on_device(): lax.all_to_all(pieces, PLANE, 0, 0, tiled=True).reshape(4, QT, 16, WIDE)  38.8 us
    pallas_call x1, Pallas kernels, bwd(): pl.pallas_call(bwd_kernel, in_specs=[SMEM] + [VMEM] * 9, out_specs=[VMEM]...  22.4 us
    pallas_call x1, Pallas kernels, fwd(): pl.pallas_call(fwd_kernel, in_specs=[SMEM] + [VMEM] * 4, out_specs=[VMEM,...  12.7 us
    all_to_all x1, starting transfers between devices, on_device(): lax.all_to_all(pieces, PLANE, 0, 0, tiled=True).reshape(4, QT, 16, WIDE)  11.6 us
    unnamed x12, local copies, waits for them, and re-layouts  5.24 us
    ppermute x3, waiting for transfers between devices, on_device(): lax.ppermute(st, 'head', [(i, (i + k) % 4) for i in range(4)])  5.17 us
  transfers between devices with their start and end apart: 6, of which 6 were waited for; matrix products, arithmetic and copies ran while one was open for 2% of the time, Pallas kernels for 0%

profile of v2, /device:TPU:0, one launch (start us, length us, event | category | flops | bytes accessed | tf_op | source)
XLA Modules:
  0.0 158.3 jit_solution(12254929583664027175)
XLA Ops:
  0.6 0.0 copy-start.1
  0.6 0.9 copy-done.1
  1.6 0.0 copy-start.2
  1.6 0.9 copy-done.2
  2.5 0.0 copy-start.3
  2.5 0.8 copy-done.3
  3.4 0.0 copy-start.4
  3.4 0.8 copy-done.4
  4.2 0.3 pack.1
  4.5 0.0 copy-start
  4.5 1.7 %copy-done = bf16[64,16,1536]{2,1,0:T(8,128)(2,1)} copy-done((bf16[64,16,1536]{2,1,0:T(8,128)(2,1)}, bf16[64,16,1536]{2,1,0:T(8,128)(2,1)S(1)}, u32[]{:S(2)}) %copy-start) | copy-done | bytes 3145752
  6.2 0.0 copy-start.5
  6.2 11.6 %all-to-all-start = ((bf16[64,16,1536]{2,1,0:T(8,128)(2,1)}), bf16[64,16,1536]{2,1,0:T(8,128)(2,1)S(1)}, u32[]{:S(2)}, u32[]{:S(2)}) async-start(bf16[64,16,1536]{2,1,0:T(8,128)(2,1)} %copy-done), calls=%async_computation | async-start | bytes 6291456 | tf_op jit(solution)/shard_map/all_to_all | solution.py:329
  17.8 0.1 and.222
  17.9 0.1 and.227
  18.0 0.1 add.207
  18.1 0.1 sub.124
  18.2 0.1 add_add_fusion
  18.3 0.1 add.204
  18.3 0.1 add.205
  18.4 0.0 copy-done.5
  18.4 0.1 select_reduce_fusion.3
  18.5 0.1 select_reduce_fusion.2
  18.6 0.2 fusion.4
  18.9 0.1 ge.95
  19.0 0.1 and.226
  19.1 0.1 convert_reduce_fusion
  19.2 0.1 convert_reduce_fusion.1
  19.3 0.2 select_reduce_fusion.1
  19.5 38.8 %all-to-all-done = bf16[64,16,1536]{2,1,0:T(8,128)(2,1)S(1)} async-done(((bf16[64,16,1536]{2,1,0:T(8,128)(2,1)}), bf16[64,16,1536]{2,1,0:T(8,128)(2,1)S(1)}, u32[]{:S(2)}, u32[]{:S(2)}) %all-to-all-start) | async-done | bytes 3145760 | tf_op jit(solution)/shard_map/all_to_all | solution.py:329
  58.3 1.1 slice.14
  59.3 0.0 collective-permute-start
  59.4 0.1 tile.18
  59.5 0.1 tile.16
  59.6 0.7 convert_reduce_fusion.3
  60.3 0.6 compare_select_fusion.1
  60.9 0.7 compare_select_fusion
  61.7 0.7 collective-permute-done.oth_ref
  62.3 0.1 broadcast_in_dim.85.kpos_ref
  62.4 12.7 %fwd.1 = (f32[16,128,256]{2,1,0:T(8,128)S(1)}, f32[16,4,256]{2,1,0:T(4,128)S(1)}) custom-call(s32[2,160]{1,0:T(2,128)S(1)} %pad_add_fusion.1.steps, s32[17,2,256]{2,1,0:T(2,128)S(1)} %pad_add_fusion.pos_ref, s32[256,128]{1,0:T(8,128)S(1)} %broadcast_in_dim.85.kpos_ref, bf16[4,16,16,1536]{3,2,1,0:T(8,128)(2,1)S(1)} %bitcast.13, ...), custom_call_target="tpu_custom_call" | custom-call | tf_op jit(solution)/shard_map/fwd/pallas_call | solution.py:196
  75.2 1.2 collective-permute-start.3
  76.4 1.5 collective-permute-start.2
  77.9 0.4 collective-permute-start.1
  78.3 1.9 %collective-permute-done.3.st3_ref = f32[16,4,256]{2,1,0:T(4,128)S(1)} collective-permute-done((f32[16,4,256]{2,1,0:T(4,128)S(1)}, f32[16,4,256]{2,1,0:T(4,128)S(1)}, u32[]{:S(2)}, u32[]{:S(2)}) %collective-permute-start.3) | collective-permute-done | bytes 65568 | tf_op jit(solution)/shard_map/ppermute | solution.py:332
  80.2 2.7 %collective-permute-done.2.st2_ref = f32[16,4,256]{2,1,0:T(4,128)S(1)} collective-permute-done((f32[16,4,256]{2,1,0:T(4,128)S(1)}, f32[16,4,256]{2,1,0:T(4,128)S(1)}, u32[]{:S(2)}, u32[]{:S(2)}) %collective-permute-start.2) | collective-permute-done | bytes 65568 | tf_op jit(solution)/shard_map/ppermute | solution.py:332
  82.9 0.6 collective-permute-done.1.st1_ref
  83.5 22.4 %bwd.1 = (bf16[4,16,16,1536]{3,2,1,0:T(8,128)(2,1)S(1)}, bf16[4,16,16,512]{3,2,1,0:T(8,128)(2,1)S(1)}) custom-call(s32[2,160]{1,0:T(2,128)S(1)} %pad_add_fusion.1.steps, s32[17,2,256]{2,1,0:T(2,128)S(1)} %pad_add_fusion.pos_ref, s32[256,128]{1,0:T(8,128)S(1)} %broadcast_in_dim.85.kpos_ref, f32[16,4,256]{2,1,0:T(4,128)S(1)} %get-tuple-element.12.st0_ref, ...), custom_call_target="tpu_custom_call" | custom-call | tf_op jit(solution)/shard_map/bwd/pallas_call | solution.py:212
  105.9 0.1 collective-permute-start.4
  106.0 2.6 %collective-permute-done.4.other_ref = bf16[4,16,16,512]{3,2,1,0:T(8,128)(2,1)S(1)} collective-permute-done((bf16[4,16,16,512]{3,2,1,0:T(8,128)(2,1)S(1)}, bf16[4,16,16,512]{3,2,1,0:T(8,128)(2,1)S(1)}, u32[]{:S(2)}, u32[]{:S(2)}) %collective-permute-start.4) | collective-permute-done | bytes 1048608 | tf_op jit(solution)/shard_map/ppermute | solution.py:334
  108.7 0.8 add_cores.1
  109.5 47.7 %all_to_all.10.in_ref = bf16[64,16,1536]{2,1,0:T(8,128)(2,1)S(1)} all-to-all(bf16[64,16,1536]{2,1,0:T(8,128)(2,1)S(1)} %bitcast.15), channel_id=1, replica_groups=mesh['head'=4,'inner'=8,'zl'=2,'core'=2] {'head','inner','zl'}, dimensions={0} | all-to-all | bytes 6291456 | tf_op jit(solution)/shard_map/all_to_all | solution.py:335
  157.2 1.1 sum_pieces.1
  (18 shorter events, 0.2 us)
Async XLA Ops:
  0.6 1.0 copy-start.1
  1.6 0.9 copy-start.2
  2.5 0.8 copy-start.3
  3.4 0.8 copy-start.4
  4.5 1.7 %copy-start = (bf16[64,16,1536]{2,1,0:T(8,128)(2,1)}, bf16[64,16,1536]{2,1,0:T(8,128)(2,1)S(1)}, u32[]{:S(2)}) copy-start(bf16[64,16,1536]{2,1,0:T(8,128)(2,1)S(1)} %pack.1) | copy-start | bytes 9437188
  6.2 12.3 %copy-start.5 = (s32[4]{0:T(128)S(1)}, s32[4]{0:T(128)}, u32[]{:S(2)}) copy-start(s32[4]{0:T(128)} %param.9) | copy-start | bytes 52
  6.2 52.1 %all-to-all-start = ((bf16[64,16,1536]{2,1,0:T(8,128)(2,1)}), bf16[64,16,1536]{2,1,0:T(8,128)(2,1)S(1)}, u32[]{:S(2)}, u32[]{:S(2)}) async-start(bf16[64,16,1536]{2,1,0:T(8,128)(2,1)} %copy-done), calls=%async_computation | async-start | bytes 6291456 | tf_op jit(solution)/shard_map/all_to_all | solution.py:329
  59.3 3.0 %collective-permute-start = (bf16[4,16,16,512]{3,2,1,0:T(8,128)(2,1)}, bf16[4,16,16,512]{3,2,1,0:T(8,128)(2,1)}, u32[]{:S(2)}, u32[]{:S(2)}) collective-permute-start(bf16[4,16,16,512]{3,2,1,0:T(8,128)(2,1)} %slice.14), channel_id=1, source_target_pairs={{0,1},{1,0},{2,3},{3,2},{4,5},{5,4},{6,7},{7,6},{8,9},{9,8},{10,11... | collective-permute-start | bytes 3145736 | tf_op jit(solution)/shard_map/ppermute | solution.py:330
  75.2 5.0 %collective-permute-start.3 = (f32[16,4,256]{2,1,0:T(4,128)S(1)}, f32[16,4,256]{2,1,0:T(4,128)S(1)}, u32[]{:S(2)}, u32[]{:S(2)}) collective-permute-start(f32[16,4,256]{2,1,0:T(4,128)S(1)} %get-tuple-element.12.st0_ref), channel_id=1, source_target_pairs={{0,96},{32,0},{64,32},{96,64},{1,97},{33,1},{65,33},{97,65},{2,98}... | collective-permute-start | bytes 196616 | tf_op jit(solution)/shard_map/ppermute | solution.py:332
  76.4 6.4 %collective-permute-start.2 = (f32[16,4,256]{2,1,0:T(4,128)S(1)}, f32[16,4,256]{2,1,0:T(4,128)S(1)}, u32[]{:S(2)}, u32[]{:S(2)}) collective-permute-start(f32[16,4,256]{2,1,0:T(4,128)S(1)} %get-tuple-element.12.st0_ref), channel_id=1, source_target_pairs={{0,64},{32,96},{64,0},{96,32},{1,65},{33,97},{65,1},{97,33},{2,66}... | collective-permute-start | bytes 196616 | tf_op jit(solution)/shard_map/ppermute | solution.py:332
  77.9 5.6 %collective-permute-start.1 = (f32[16,4,256]{2,1,0:T(4,128)S(1)}, f32[16,4,256]{2,1,0:T(4,128)S(1)}, u32[]{:S(2)}, u32[]{:S(2)}) collective-permute-start(f32[16,4,256]{2,1,0:T(4,128)S(1)} %get-tuple-element.12.st0_ref), channel_id=1, source_target_pairs={{0,32},{32,64},{64,96},{96,0},{1,33},{33,65},{65,97},{97,1},{2,34}... | collective-permute-start | bytes 196616 | tf_op jit(solution)/shard_map/ppermute | solution.py:332
  105.9 2.7 %collective-permute-start.4 = (bf16[4,16,16,512]{3,2,1,0:T(8,128)(2,1)S(1)}, bf16[4,16,16,512]{3,2,1,0:T(8,128)(2,1)S(1)}, u32[]{:S(2)}, u32[]{:S(2)}) collective-permute-start(bf16[4,16,16,512]{3,2,1,0:T(8,128)(2,1)S(1)} %get-tuple-element.15), channel_id=1, source_target_pairs={{0,1},{1,0},{2,3},{3,2},{4,5},{5,4},{6,7},{7,6},{8,9},{9,8},{10,11... | collective-permute-start | bytes 3145736 | tf_op jit(solution)/shard_map/ppermute | solution.py:334

commit v3 on v2

--- a/solution.py
+++ b/solution.py
@@ -13,7 +13,7 @@
 QT = 16
 KP = 16
 LIST = 160
-WIDE = 1536
+WIDE = 1024
 bf16, f32, i32 = jnp.bfloat16, jnp.float32, jnp.int32
 VMEM = pl.BlockSpec(memory_space=pltpu.VMEM)
 SMEM = pl.BlockSpec(memory_space=pltpu.SMEM)
@@ -33,7 +33,7 @@
 
 
 def key_tile(own_ref, oth_ref, p, first):
-    parts = [own_ref[:, p, :, 1024 + 256 * h + first:1024 + 256 * h + first + HD].reshape(64, HD) for h in (0, 1)]
+    parts = [own_ref[:, p, :, 512 + 256 * h + first:512 + 256 * h + first + HD].reshape(64, HD) for h in (0, 1)]
     parts += [oth_ref[:, p, :, 256 * h + first:256 * h + first + HD].reshape(64, HD) for h in (0, 1)]
     return jnp.concatenate(parts, axis=0)
 
@@ -120,15 +120,16 @@
         ot_ref[n] = o
         st_ref[n, 0:1, :] = m_s[n]
         st_ref[n, 1:2, :] = l_s[n]
-        st_ref[n, 2:3, :] = jnp.sum(row_tile(own_ref, n, 512).T.astype(f32) * o, axis=0, keepdims=True)
-
-
-def bwd_kernel(steps, pos_ref, kpos_ref, st0_ref, st1_ref, st2_ref, st3_ref, own_ref, oth_ref, ot_ref,
-               out_ref, oth_out_ref, kt, lse_s, delta_s, w_s, dq, dk, dv, s_buf, dp_buf, p_buf, ds_buf):
-    @pl.loop(0, KP, unroll=4)
-    def _(p):
-        kt[:, pl.ds(pl.multiple_of(p * 256, 256), 256)] = key_tile(own_ref, oth_ref, p, 0).T
-
+
+
+def delta_kernel(st_ref, ot_ref, do_ref, out_ref):
+    @pl.loop(0, QT, unroll=4)
+    def _(n):
+        out_ref[n, 0:2, :] = st_ref[n, 0:2, :]
+        out_ref[n, 2:3, :] = jnp.sum(row_tile(do_ref, n, 0).T.astype(f32) * ot_ref[n], axis=0, keepdims=True)
+
+
+def scale_kernel(st0_ref, st1_ref, st2_ref, st3_ref, ot_ref, stat_ref, out_ref):
     refs = (st0_ref, st1_ref, st2_ref, st3_ref)
 
     @pl.loop(0, QT, unroll=4)
@@ -138,11 +139,21 @@
             top = jnp.maximum(top, ref[n, 0:1, :])
         share = [jnp.exp2(ref[n, 0:1, :] - top) for ref in refs]
         total = sum(w * ref[n, 1:2, :] for w, ref in zip(share, refs))
-        lse_s[n] = top + jnp.log2(total)
-        delta_s[n] = sum(w * ref[n, 2:3, :] for w, ref in zip(share, refs)) / total
-        w_s[n] = share[0] / total
-    lse_s[QT] = jnp.full((1, 256), -NEG, f32)
-    delta_s[QT] = jnp.zeros((1, 256), f32)
+        stat_ref[n, 0:1, :] = top + jnp.log2(total)
+        stat_ref[n, 1:2, :] = sum(w * ref[n, 2:3, :] for w, ref in zip(share, refs)) / total
+        ob = (ot_ref[n] * (share[0] / total)).astype(bf16).T
+        for h in range(4):
+            out_ref[:, n, :, h * HD:(h + 1) * HD] = ob[h * 64:(h + 1) * 64].reshape(4, 16, HD)
+    stat_ref[QT, 0:1, :] = jnp.full((1, 256), -NEG, f32)
+    stat_ref[QT, 1:2, :] = jnp.zeros((1, 256), f32)
+
+
+def bwd_kernel(steps, pos_ref, kpos_ref, stat_ref, own_ref, oth_ref, do_ref, out_ref, oth_out_ref,
+               kt, dq, dk, dv, s_buf, dp_buf, p_buf, ds_buf):
+    @pl.loop(0, KP, unroll=4)
+    def _(p):
+        kt[:, pl.ds(pl.multiple_of(p * 256, 256), 256)] = key_tile(own_ref, oth_ref, p, 0).T
+
     dq[...] = jnp.zeros_like(dq)
     dk[...] = jnp.zeros_like(dk)
     dv[...] = jnp.zeros_like(dv)
@@ -152,18 +163,18 @@
             n, p = unpack(steps, kind, t)
             s = nt(key_tile(own_ref, oth_ref, p, 0), row_tile(own_ref, n, 0)) * SC2
             s_buf[buf] = mask_scores(s, n, p, pos_ref, kpos_ref, NEG) if kind else s
-            dp_buf[buf] = nt(key_tile(own_ref, oth_ref, p, HD), row_tile(own_ref, n, 512))
+            dp_buf[buf] = nt(key_tile(own_ref, oth_ref, p, HD), row_tile(do_ref, n, 0))
 
         def soften(t, buf):
             n, _ = unpack(steps, kind, t)
-            w = jnp.exp2(s_buf[buf] - lse_s[n])
+            w = jnp.exp2(s_buf[buf] - stat_ref[n, 0:1, :])
             p_buf[buf] = w.astype(bf16)
-            ds_buf[buf] = (w * (dp_buf[buf] - delta_s[n])).astype(bf16)
+            ds_buf[buf] = (w * (dp_buf[buf] - stat_ref[n, 1:2, :])).astype(bf16)
 
         def gather(t, buf):
             n, p = unpack(steps, kind, t)
             ds = ds_buf[buf]
-            dv[p] += nn(p_buf[buf], row_tile(own_ref, n, 512))
+            dv[p] += nn(p_buf[buf], row_tile(do_ref, n, 0))
             dk[p] += nn(ds, row_tile(own_ref, n, 0))
             dq[n] += nn(lanes_at(kt, p), ds)
 
@@ -177,18 +188,16 @@
 
     @pl.loop(0, QT, unroll=4)
     def _(n):
-        ob = (ot_ref[n] * w_s[n]).astype(bf16).T
         qb = (dq[n] * SCALE).astype(bf16).T
         for h in range(4):
-            out_ref[:, n, :, h * HD:(h + 1) * HD] = ob[h * 64:(h + 1) * 64].reshape(4, 16, HD)
-            out_ref[:, n, :, 512 + h * HD:512 + (h + 1) * HD] = qb[h * 64:(h + 1) * 64].reshape(4, 16, HD)
+            out_ref[:, n, :, h * HD:(h + 1) * HD] = qb[h * 64:(h + 1) * 64].reshape(4, 16, HD)
 
     @pl.loop(0, KP, unroll=4)
     def _(p):
         for first, tile in ((0, (dk[p] * SCALE).astype(bf16)), (HD, dv[p].astype(bf16))):
             for h in (0, 1):
                 at = 256 * h + first
-                out_ref[:, p, :, 1024 + at:1024 + at + HD] = tile[64 * h:64 * h + 64].reshape(4, 16, HD)
+                out_ref[:, p, :, 512 + at:512 + at + HD] = tile[64 * h:64 * h + 64].reshape(4, 16, HD)
                 oth_out_ref[:, p, :, at:at + HD] = tile[128 + 64 * h:192 + 64 * h].reshape(4, 16, HD)
 
 
@@ -204,47 +213,102 @@
         ],
         out_shape=[jax.ShapeDtypeStruct((QT, HD, 256), f32), jax.ShapeDtypeStruct((QT, 4, 256), f32)],
         compiler_params=pltpu.CompilerParams(vmem_limit_bytes=16 << 20),
+        cost_estimate=pl.CostEstimate(flops=15 * 10 ** 9, bytes_accessed=8 << 20, transcendentals=0),
         name="fwd",
     )(steps, pos, kpos, own, oth)
 
 
-def bwd(steps, pos, kpos, sts, own, oth, ot):
+def delta(st, ot, do):
+    return pl.pallas_call(
+        delta_kernel, in_specs=[VMEM] * 3, out_specs=VMEM, out_shape=jax.ShapeDtypeStruct((QT, 4, 256), f32),
+        compiler_params=pltpu.CompilerParams(vmem_limit_bytes=12 << 20), name="delta",
+    )(st, ot, do)
+
+
+def scale(sts, ot):
+    return pl.pallas_call(
+        scale_kernel, in_specs=[VMEM] * 5, out_specs=[VMEM] * 2,
+        out_shape=[jax.ShapeDtypeStruct((QT + 1, 2, 256), f32), jax.ShapeDtypeStruct((4, QT, 16, 512), bf16)],
+        compiler_params=pltpu.CompilerParams(vmem_limit_bytes=12 << 20), name="scale",
+    )(*sts, ot)
+
+
+def bwd(steps, pos, kpos, stat, own, oth, do):
     return pl.pallas_call(
         bwd_kernel,
-        in_specs=[SMEM] + [VMEM] * 9,
+        in_specs=[SMEM] + [VMEM] * 6,
         out_specs=[VMEM] * 2,
         scratch_shapes=[
             pltpu.VMEM((HD, KP * 256), bf16),
-            pltpu.VMEM((QT + 1, 1, 256), f32), pltpu.VMEM((QT + 1, 1, 256), f32), pltpu.VMEM((QT + 1, 1, 256), f32),
             pltpu.VMEM((QT + 1, HD, 256), f32), pltpu.VMEM((KP, 256, HD), f32), pltpu.VMEM((KP, 256, HD), f32),
             pltpu.VMEM((4, 256, 256), f32), pltpu.VMEM((4, 256, 256), f32),
             pltpu.VMEM((4, 256, 256), bf16), pltpu.VMEM((4, 256, 256), bf16),
         ],
         out_shape=[jax.ShapeDtypeStruct((4, QT, 16, WIDE), bf16), jax.ShapeDtypeStruct((4, KP, 16, 512), bf16)],
         compiler_params=pltpu.CompilerParams(vmem_limit_bytes=24 << 20),
+        cost_estimate=pl.CostEstimate(flops=25 * 10 ** 9, bytes_accessed=8 << 20, transcendentals=0),
         name="bwd",
-    )(steps, pos, kpos, *sts, own, oth, ot)
-
-
-def pack_kernel(q_ref, k_ref, v_ref, do_ref, out_ref):
+    )(steps, pos, kpos, stat, own, oth, do)
+
+
+def pack_kernel(q_hbm, k_hbm, v_hbm, out_hbm, q_ref, k_ref, v_ref, out_ref, in_sem, out_sem):
+    loads = [pltpu.make_async_copy(src, dst, in_sem.at[i])
+             for i, (src, dst) in enumerate(((q_hbm, q_ref), (k_hbm, k_ref), (v_hbm, v_ref)))]
+    for load in loads:
+        load.start()
+    for load in loads:
+        load.wait()
+    stores = []
     for j in range(4):
         for u in range(8):
             for g in range(2):
-                at = j * 16 + u * 2 + g
-                out_ref[at, :, 0:512] = q_ref[16 * u:16 * u + 16, 512 * g:512 * g + 512]
-                out_ref[at, :, 512:1024] = do_ref[16 * u:16 * u + 16, 512 * g:512 * g + 512]
+                at = u * 2 + g
+                out_ref[j, at, :, 0:512] = q_ref[16 * u:16 * u + 16, 512 * g:512 * g + 512]
                 for h in (0, 1):
                     rows = slice(32 * j + 16 * h, 32 * j + 16 * h + 16)
-                    out_ref[at, :, 1024 + 256 * h:1152 + 256 * h] = k_ref[rows, HD * g:HD * g + HD]
-                    out_ref[at, :, 1152 + 256 * h:1280 + 256 * h] = v_ref[rows, HD * g:HD * g + HD]
-
-
-def pack(q, k, v, do):
-    return pl.pallas_call(
-        pack_kernel, in_specs=[VMEM] * 4, out_specs=VMEM,
-        out_shape=jax.ShapeDtypeStruct((64, 16, WIDE), bf16),
-        compiler_params=pltpu.CompilerParams(vmem_limit_bytes=12 << 20), name="pack",
-    )(q, k, v, do)
+                    out_ref[j, at, :, 512 + 256 * h:640 + 256 * h] = k_ref[rows, HD * g:HD * g + HD]
+                    out_ref[j, at, :, 640 + 256 * h:768 + 256 * h] = v_ref[rows, HD * g:HD * g + HD]
+        stores.append(pltpu.make_async_copy(out_ref.at[j], out_hbm.at[j], out_sem.at[j]))
+        stores[-1].start()
+    for store in stores:
+        store.wait()
+
+
+def pack(q, k, v):
+    any_spec = pl.BlockSpec(memory_space=pltpu.HBM)
+    return pl.pallas_call(
+        pack_kernel, in_specs=[any_spec] * 3, out_specs=any_spec,
+        out_shape=jax.ShapeDtypeStruct((4, 16, 16, WIDE), bf16),
+        scratch_shapes=[pltpu.VMEM((128, 1024), bf16), pltpu.VMEM((128, 256), bf16), pltpu.VMEM((128, 256), bf16),
+                        pltpu.VMEM((4, 16, 16, WIDE), bf16), pltpu.SemaphoreType.DMA((3,)), pltpu.SemaphoreType.DMA((4,))],
+        compiler_params=pltpu.CompilerParams(vmem_limit_bytes=60 << 20), name="pack",
+    )(q, k, v)
+
+
+def spread_kernel(do_ref, out_ref):
+    for j in range(4):
+        for u in range(8):
+            for g in range(2):
+                out_ref[j * 16 + u * 2 + g] = do_ref[16 * u:16 * u + 16, 512 * g:512 * g + 512]
+
+
+def spread(do):
+    return pl.pallas_call(
+        spread_kernel, in_specs=[VMEM], out_specs=VMEM, out_shape=jax.ShapeDtypeStruct((64, 16, 512), bf16),
+        compiler_params=pltpu.CompilerParams(vmem_limit_bytes=12 << 20), name="spread",
+    )(do)
+
+
+def pass_kernel(*refs):
+    del refs
+
+
+def pass_after(x, earlier):
+    any_spec = pl.BlockSpec(memory_space=pl.ANY)
+    return pl.pallas_call(
+        pass_kernel, in_specs=[any_spec] * 2, out_specs=any_spec, out_shape=jax.ShapeDtypeStruct(x.shape, x.dtype),
+        input_output_aliases={0: 0}, name="pass_after",
+    )(x, earlier)
 
 
 def add_kernel(own_ref, other_ref, out_ref):
@@ -252,7 +316,7 @@
 
 
 def add_other(out, other):
-    last = pl.BlockSpec((4, KP, 16, 512), lambda i: (0, 0, 0, 2))
+    last = pl.BlockSpec((4, KP, 16, 512), lambda i: (0, 0, 0, 1))
     return pl.pallas_call(
         add_kernel, grid=(1,), in_specs=[last, pl.BlockSpec((4, KP, 16, 512), lambda i: (0, 0, 0, 0))], out_specs=last,
         out_shape=jax.ShapeDtypeStruct(out.shape, bf16), input_output_aliases={0: 0},
@@ -260,27 +324,36 @@
     )(out, other)
 
 
-def sum_kernel(in_ref, at_ref, qg_ref, kg_ref, vg_ref):
+def sum_rows(in_ref, out_ref):
     for u in range(8):
         for g in range(2):
-            rows, cols = slice(16 * u, 16 * u + 16), slice(512 * g, 512 * g + 512)
-            for first, ref in ((0, at_ref), (512, qg_ref)):
-                parts = [in_ref[j * 16 + u * 2 + g, :, first:first + 512].astype(f32) for j in range(4)]
-                ref[rows, cols] = (parts[0] + parts[1] + parts[2] + parts[3]).astype(bf16)
+            parts = [in_ref[j * 16 + u * 2 + g, :, 0:512].astype(f32) for j in range(4)]
+            out_ref[16 * u:16 * u + 16, 512 * g:512 * g + 512] = (parts[0] + parts[1] + parts[2] + parts[3]).astype(bf16)
+
+
+def sum_attended(pieces):
+    return pl.pallas_call(
+        sum_rows, in_specs=[VMEM], out_specs=VMEM, out_shape=jax.ShapeDtypeStruct((128, 1024), bf16),
+        compiler_params=pltpu.CompilerParams(vmem_limit_bytes=12 << 20), name="sum_attended",
+    )(pieces)
+
+
+def sum_kernel(in_ref, qg_ref, kg_ref, vg_ref):
+    sum_rows(in_ref, qg_ref)
     for j in range(4):
         for g in range(2):
             for h in (0, 1):
                 rows, cols = slice(32 * j + 16 * h, 32 * j + 16 * h + 16), slice(HD * g, HD * g + HD)
-                both = sum(in_ref[j * 16 + u * 2 + g, :, 1024 + 256 * h:1280 + 256 * h].astype(f32) for u in range(8))
+                both = sum(in_ref[j * 16 + u * 2 + g, :, 512 + 256 * h:768 + 256 * h].astype(f32) for u in range(8))
                 kg_ref[rows, cols] = both[:, :HD].astype(bf16)
                 vg_ref[rows, cols] = both[:, HD:].astype(bf16)
 
 
-def sum_pieces(pieces):
+def sum_grads(pieces):
     big, small = jax.ShapeDtypeStruct((128, 1024), bf16), jax.ShapeDtypeStruct((128, 256), bf16)
     return pl.pallas_call(
-        sum_kernel, in_specs=[VMEM], out_specs=[VMEM] * 4, out_shape=[big, big, small, small],
-        compiler_params=pltpu.CompilerParams(vmem_limit_bytes=12 << 20), name="sum_pieces",
+        sum_kernel, in_specs=[VMEM], out_specs=[VMEM] * 3, out_shape=[big, small, small],
+        compiler_params=pltpu.CompilerParams(vmem_limit_bytes=12 << 20), name="sum_grads",
     )(pieces)
 
 
@@ -324,16 +397,21 @@
     j, u, core = (lax.axis_index(name) for name in ("head", "inner", "core"))
     swap = [(0, 1), (1, 0)]
     steps, pos, kpos = make_plan(lengths, core, u, j)
-    pieces = pack(query_rows.reshape(128, 1024), key_rows.reshape(128, 256), value_rows.reshape(128, 256),
-                  out_grad.reshape(128, 1024))
-    own = lax.all_to_all(pieces, PLANE, 0, 0, tiled=True).reshape(4, QT, 16, WIDE)
-    oth = lax.ppermute(own[..., 1024:], "core", swap)
+    pieces = pack(query_rows.reshape(128, 1024), key_rows.reshape(128, 256), value_rows.reshape(128, 256))
+    own = lax.all_to_all(pieces.reshape(64, 16, WIDE), PLANE, 0, 0, tiled=True)
+    own = own.reshape(4, QT, 16, WIDE)
+    do = lax.all_to_all(spread(out_grad.reshape(128, 1024)), PLANE, 0, 0, tiled=True).reshape(4, QT, 16, 512)
+    oth = lax.ppermute(own[..., 512:], "core", swap)
     ot, st = fwd(steps, pos, kpos, own, oth)
+    st = delta(st, ot, do)
     sts = [st] + [lax.ppermute(st, "head", [(i, (i + k) % 4) for i in range(4)]) for k in (1, 2, 3)]
-    out, oth_out = bwd(steps, pos, kpos, sts, own, oth, ot)
-    out = add_other(out, lax.ppermute(oth_out, "core", swap))
+    stat, scaled = scale(sts, ot)
+    scaled = lax.all_to_all(scaled.reshape(64, 16, 512), PLANE, 0, 0, tiled=True)
+    out, oth_out = bwd(steps, pos, kpos, stat, own, oth, do)
+    out = add_other(out, lax.ppermute(pass_after(oth_out, scaled), "core", swap))
     out = lax.all_to_all(out.reshape(64, 16, WIDE), PLANE, 0, 0, tiled=True)
-    attended, query_grad, key_grad, value_grad = sum_pieces(out)
+    attended = sum_attended(scaled)
+    query_grad, key_grad, value_grad = sum_grads(out)
     return (attended.reshape(1, 1, 128, 1024), query_grad.reshape(1, 1, 128, 1024),
             key_grad.reshape(1, 1, 128, 256), value_grad.reshape(1, 1, 128, 256))
 

time: 161 us -> 162 us (level); the launches traced: 158 us -> 161 us
  blocking collectives: 47.7 us -> 0 us
  starting transfers between devices: 14.8 us -> 40 us
  waiting for transfers between devices: 47.3 us -> 65 us
  Pallas kernels: 37.4 us -> 43.2 us
  local copies, waits for them, and re-layouts: 7.27 us -> 9.19 us
    all_to_all x1 -> x0, blocking collectives: 47.7 us -> none  [on_device(): out = lax.all_to_all(out.reshape(64, 16, WIDE), PLANE, 0, 0, tiled=True)]
    all_to_all x1 -> x4, starting transfers between devices: 11.6 us -> 35.6 us  [the longest x1 11.6 us: on_device(): own = lax.all_to_all(pieces.reshape(64, 16, WIDE), PLANE, 0, 0, tiled=True)]
    all_to_all x1 -> x4, waiting for transfers between devices: 38.8 us -> 56.3 us  [the longest x1 29.1 us: on_device(): out = lax.all_to_all(out.reshape(64, 16, WIDE), PLANE, 0, 0, tiled=True)]
    pallas_call x3 -> x8, Pallas kernels: 23.8 us -> 28.6 us  [the longest x1 23.2 us: bwd(): pl.pallas_call(bwd_kernel, in_specs=[SMEM] + [VMEM] * 6, out_specs=[VMEM]...]
    unnamed x12 -> x20, local copies, waits for them, and re-layouts: 5.24 us -> 7.11 us
    pallas_call x1, Pallas kernels: 0.83 us -> 2.52 us  [add_other(): pl.pallas_call(add_kernel, grid=(1,), in_specs=[last, pl.BlockSpec((4, KP...]
  transfers between devices with their start and end apart: 6 -> 9, of which waited for: 6 -> 8; matrix products, arithmetic and copies ran while one was open for 2% -> 3% of each run, Pallas kernels for 0% -> 22%
where the time goes in v3:
time: 162 us; the launch traced here: 161 us
  waiting for transfers between devices  65 us (40%)
  Pallas kernels  43.2 us (27%)
  starting transfers between devices  40 us (25%)
  local copies, waits for them, and re-layouts  9.19 us (6%)
  other arithmetic  2.97 us (2%)
    all_to_all x1, waiting for transfers between devices, on_device(): out = lax.all_to_all(out.reshape(64, 16, WIDE), PLANE, 0, 0, tiled=True)  29.1 us
    all_to_all x1, waiting for transfers between devices, on_device(): own = lax.all_to_all(pieces.reshape(64, 16, WIDE), PLANE, 0, 0, tiled=True)  26.9 us
    pallas_call x1, Pallas kernels, bwd(): pl.pallas_call(bwd_kernel, in_specs=[SMEM] + [VMEM] * 6, out_specs=[VMEM]...  23.2 us
    pallas_call x1, Pallas kernels, fwd(): pl.pallas_call(fwd_kernel, in_specs=[SMEM] + [VMEM] * 4, out_specs=[VMEM,...  12.1 us
    all_to_all x1, starting transfers between devices, on_device(): own = lax.all_to_all(pieces.reshape(64, 16, WIDE), PLANE, 0, 0, tiled=True)  11.6 us
    all_to_all x1, starting transfers between devices, on_device(): out = lax.all_to_all(out.reshape(64, 16, WIDE), PLANE, 0, 0, tiled=True)  10.5 us
    all_to_all x1, starting transfers between devices, on_device(): lax.all_to_all(scaled.reshape(64, 16, 512), PLANE, 0, 0, tiled=True)  8.21 us
    unnamed x20, local copies, waits for them, and re-layouts  7.11 us
  transfers between devices with their start and end apart: 9, of which 8 were waited for; matrix products, arithmetic and copies ran while one was open for 3% of the time, Pallas kernels for 22%

profile of v3, /device:TPU:0, one launch (start us, length us, event | category | flops | bytes accessed | tf_op | source)
XLA Modules:
  0.0 161.3 jit_solution(14132585006816733872)
XLA Ops:
  0.6 2.4 %pack.1 = bf16[4,16,16,1024]{3,2,1,0:T(8,128)(2,1)} custom-call(bf16[128,1024]{1,0:T(8,128)(2,1)} %bitcast.23, bf16[128,256]{1,0:T(8,128)(2,1)} %bitcast.25, bf16[128,256]{1,0:T(8,128)(2,1)} %bitcast.26), custom_call_target="tpu_custom_call" | custom-call | tf_op jit(solution)/shard_map/pack/pallas_call | solution.py:279
  3.1 0.0 copy-start.9
  3.1 0.0 copy-start.8
  3.1 11.6 %all-to-all-start = ((bf16[64,16,1024]{2,1,0:T(8,128)(2,1)}), bf16[64,16,1024]{2,1,0:T(8,128)(2,1)S(1)}, u32[]{:S(2)}, u32[]{:S(2)}) async-start(bf16[64,16,1024]{2,1,0:T(8,128)(2,1)} %bitcast.22), calls=%async_computation | async-start | bytes 4194304 | tf_op jit(solution)/shard_map/all_to_all | solution.py:401
  14.8 0.1 add_add_fusion
  14.9 0.1 and.222
  14.9 0.1 and.227
  15.0 0.1 add.207
  15.1 0.1 sub.124
  15.2 0.1 add.204
  15.3 0.1 add.205
  15.4 0.0 copy-done.9
  15.4 0.1 select_reduce_fusion.3
  15.5 0.1 select_reduce_fusion.2
  15.6 0.2 fusion.4
  15.8 0.1 ge.95
  15.9 0.1 and.226
  16.0 0.0 copy-done.8
  16.0 0.1 spread.1
  16.1 0.0 copy-start.5
  16.1 1.0 copy-done.5
  17.1 0.1 convert_reduce_fusion
  17.2 0.1 convert_reduce_fusion.1
  17.3 0.2 select_reduce_fusion.1
  17.5 26.9 %all-to-all-done = bf16[64,16,1024]{2,1,0:T(8,128)(2,1)S(1)} async-done(((bf16[64,16,1024]{2,1,0:T(8,128)(2,1)}), bf16[64,16,1024]{2,1,0:T(8,128)(2,1)S(1)}, u32[]{:S(2)}, u32[]{:S(2)}) %all-to-all-start) | async-done | bytes 2097184 | tf_op jit(solution)/shard_map/all_to_all | solution.py:401
  44.4 5.2 %all-to-all-start.1 = ((bf16[64,16,512]{2,1,0:T(8,128)(2,1)}), bf16[64,16,512]{2,1,0:T(8,128)(2,1)S(1)}, u32[]{:S(2)}, u32[]{:S(2)}) async-start(bf16[64,16,512]{2,1,0:T(8,128)(2,1)} %copy-done.5), calls=%async_computation.1 | async-start | bytes 2097152 | tf_op jit(solution)/shard_map/all_to_all | solution.py:403
  49.7 1.1 slice.14
  50.8 0.0 copy-done.2
  50.8 0.0 collective-permute-start
  50.8 0.1 tile.18
  50.9 0.1 tile.16
  51.0 0.7 convert_reduce_fusion.3
  51.7 0.6 compare_select_fusion.1
  52.4 0.7 compare_select_fusion
  53.1 0.7 collective-permute-done.oth_ref
  53.8 0.1 broadcast_in_dim.85.kpos_ref
  53.9 0.0 copy-start.3
  53.9 1.6 copy-done.3
  55.5 12.1 %fwd.1 = (f32[16,128,256]{2,1,0:T(8,128)S(1)}, f32[16,4,256]{2,1,0:T(4,128)S(1)}) custom-call(s32[2,160]{1,0:T(2,128)S(1)} %pad_add_fusion.1.steps, s32[17,2,256]{2,1,0:T(2,128)S(1)} %pad_add_fusion.pos_ref, s32[256,128]{1,0:T(8,128)S(1)} %broadcast_in_dim.85.kpos_ref, bf16[4,16,16,1024]{3,2,1,0:T(8,128)(2,1)S(1)} %bitcast.16, ...), custom_call_target="tpu_custom_call" | custom-call | flops 15000000512 | bytes 8388608 | tf_op jit(solution)/shard_map/fwd/pallas_call | solution.py:205
  67.6 0.2 all-to-all-done.1
  67.8 0.5 delta.1.st0_ref
  68.3 2.9 %collective-permute-start.3 = (f32[16,4,256]{2,1,0:T(4,128)S(1)}, f32[16,4,256]{2,1,0:T(4,128)S(1)}, u32[]{:S(2)}, u32[]{:S(2)}) collective-permute-start(f32[16,4,256]{2,1,0:T(4,128)S(1)} %delta.1.st0_ref), channel_id=1, source_target_pairs={{0,96},{32,0},{64,32},{96,64},{1,97},{33,1},{65,33},{97,65},{2,98}... | collective-permute-start | bytes 196616 | tf_op jit(solution)/shard_map/ppermute | solution.py:407
  71.2 0.6 collective-permute-start.2
  71.9 1.0 collective-permute-start.1
  72.8 1.5 collective-permute-done.3.st3_ref
  74.3 3.0 %collective-permute-done.2.st2_ref = f32[16,4,256]{2,1,0:T(4,128)S(1)} collective-permute-done((f32[16,4,256]{2,1,0:T(4,128)S(1)}, f32[16,4,256]{2,1,0:T(4,128)S(1)}, u32[]{:S(2)}, u32[]{:S(2)}) %collective-permute-start.2) | collective-permute-done | bytes 65568 | tf_op jit(solution)/shard_map/ppermute | solution.py:407
  77.3 0.7 collective-permute-done.1.st1_ref
  78.0 0.6 scale.1
  78.6 0.0 copy-start.7
  78.6 1.0 copy-done.7
  79.5 8.2 %all-to-all-start.2 = ((bf16[64,16,512]{2,1,0:T(8,128)(2,1)}), bf16[64,16,512]{2,1,0:T(8,128)(2,1)S(1)}, u32[]{:S(2)}, u32[]{:S(2)}) async-start(bf16[64,16,512]{2,1,0:T(8,128)(2,1)} %bitcast.20), calls=%async_computation.2 | async-start | bytes 2097152 | tf_op jit(solution)/shard_map/all_to_all | solution.py:409
  87.7 0.0 copy-start.4
  87.8 1.6 copy-done.4
  89.3 23.2 %bwd.1 = (bf16[4,16,16,1024]{3,2,1,0:T(8,128)(2,1)}, bf16[4,16,16,512]{3,2,1,0:T(8,128)(2,1)S(1)}) custom-call(s32[2,160]{1,0:T(2,128)S(1)} %pad_add_fusion.1.steps, s32[17,2,256]{2,1,0:T(2,128)S(1)} %pad_add_fusion.pos_ref, s32[256,128]{1,0:T(8,128)S(1)} %broadcast_in_dim.85.kpos_ref, f32[17,2,256]{2,1,0:T(2,128)S(1)} %get-tuple-element.16.stat_ref, ...), custom_call_target="tpu_custom_call" | custom-call | flops 24999999488 | bytes 8388608 | tf_op jit(solution)/shard_map/bwd/pallas_call | solution.py:237
  112.6 1.0 copy-done.6
  113.6 0.0 all-to-all-done.2.in_ref.refs_1_
  113.6 1.0 copy-done
  114.6 0.0 collective-permute-start.4
  114.6 2.9 %collective-permute-done.4.other_ref = bf16[4,16,16,512]{3,2,1,0:T(8,128)(2,1)S(1)} collective-permute-done((bf16[4,16,16,512]{3,2,1,0:T(8,128)(2,1)}, bf16[4,16,16,512]{3,2,1,0:T(8,128)(2,1)S(1)}, u32[]{:S(2)}, u32[]{:S(2)}) %collective-permute-start.4) | collective-permute-done | bytes 1048608 | tf_op jit(solution)/shard_map/ppermute | solution.py:411
  117.4 2.5 %add_cores.1 = bf16[4,16,16,1024]{3,2,1,0:T(8,128)(2,1)} custom-call(bf16[4,16,16,1024]{3,2,1,0:T(8,128)(2,1)} %get-tuple-element.17.own_ref, bf16[4,16,16,512]{3,2,1,0:T(8,128)(2,1)S(1)} %collective-permute-done.4.other_ref), custom_call_target="tpu_custom_call", output_to_operand_aliasing={{}: (0, {})} | custom-call | tf_op jit(solution)/shard_map/add_cores/pallas_call | solution.py:320
  120.0 10.5 %all-to-all-start.3 = ((bf16[64,16,1024]{2,1,0:T(8,128)(2,1)}), bf16[64,16,1024]{2,1,0:T(8,128)(2,1)S(1)}, u32[]{:S(2)}, u32[]{:S(2)}) async-start(bf16[64,16,1024]{2,1,0:T(8,128)(2,1)} %bitcast.11), calls=%async_computation.3 | async-start | bytes 4194304 | tf_op jit(solution)/shard_map/all_to_all | solution.py:412
  130.4 0.8 sum_attended.1
  131.3 29.1 %all-to-all-done.3.in_ref = bf16[64,16,1024]{2,1,0:T(8,128)(2,1)S(1)} async-done(((bf16[64,16,1024]{2,1,0:T(8,128)(2,1)}), bf16[64,16,1024]{2,1,0:T(8,128)(2,1)S(1)}, u32[]{:S(2)}, u32[]{:S(2)}) %all-to-all-start.3) | async-done | bytes 2097184 | tf_op jit(solution)/shard_map/all_to_all | solution.py:412
  160.4 0.9 sum_grads.1
  (24 shorter events, 0.2 us)
Async XLA Ops:
  3.1 12.3 %copy-start.9 = (s32[4]{0:T(128)S(1)}, s32[4]{0:T(128)}, u32[]{:S(2)}) copy-start(s32[4]{0:T(128)} %param.9) | copy-start | bytes 52
  3.1 12.9 %copy-start.8 = (bf16[1,1,128,1024]{3,2,1,0:T(8,128)(2,1)S(1)}, bf16[1,1,128,1024]{3,2,1,0:T(8,128)(2,1)}, u32[]{:S(2)}) copy-start(bf16[1,1,128,1024]{3,2,1,0:T(8,128)(2,1)} %param.8) | copy-start | bytes 786436
  3.1 41.3 %all-to-all-start = ((bf16[64,16,1024]{2,1,0:T(8,128)(2,1)}), bf16[64,16,1024]{2,1,0:T(8,128)(2,1)S(1)}, u32[]{:S(2)}, u32[]{:S(2)}) async-start(bf16[64,16,1024]{2,1,0:T(8,128)(2,1)} %bitcast.22), calls=%async_computation | async-start | bytes 4194304 | tf_op jit(solution)/shard_map/all_to_all | solution.py:401
  16.1 1.0 copy-start.5
  44.4 6.4 %copy-start.2 = (bf16[64,16,1024]{2,1,0:T(8,128)(2,1)}, bf16[64,16,1024]{2,1,0:T(8,128)(2,1)S(1)}, u32[]{:S(2)}) copy-start(bf16[64,16,1024]{2,1,0:T(8,128)(2,1)S(1)} %all-to-all-done) | copy-start | bytes 6291460
  44.4 23.4 %all-to-all-start.1 = ((bf16[64,16,512]{2,1,0:T(8,128)(2,1)}), bf16[64,16,512]{2,1,0:T(8,128)(2,1)S(1)}, u32[]{:S(2)}, u32[]{:S(2)}) async-start(bf16[64,16,512]{2,1,0:T(8,128)(2,1)} %copy-done.5), calls=%async_computation.1 | async-start | bytes 2097152 | tf_op jit(solution)/shard_map/all_to_all | solution.py:403
  50.8 3.0 %collective-permute-start = (bf16[4,16,16,512]{3,2,1,0:T(8,128)(2,1)}, bf16[4,16,16,512]{3,2,1,0:T(8,128)(2,1)}, u32[]{:S(2)}, u32[]{:S(2)}) collective-permute-start(bf16[4,16,16,512]{3,2,1,0:T(8,128)(2,1)} %slice.14), channel_id=1, source_target_pairs={{0,1},{1,0},{2,3},{3,2},{4,5},{5,4},{6,7},{7,6},{8,9},{9,8},{10,11... | collective-permute-start | bytes 3145736 | tf_op jit(solution)/shard_map/ppermute | solution.py:404
  53.9 1.6 copy-start.3
  68.3 6.0 %collective-permute-start.3 = (f32[16,4,256]{2,1,0:T(4,128)S(1)}, f32[16,4,256]{2,1,0:T(4,128)S(1)}, u32[]{:S(2)}, u32[]{:S(2)}) collective-permute-start(f32[16,4,256]{2,1,0:T(4,128)S(1)} %delta.1.st0_ref), channel_id=1, source_target_pairs={{0,96},{32,0},{64,32},{96,64},{1,97},{33,1},{65,33},{97,65},{2,98}... | collective-permute-start | bytes 196616 | tf_op jit(solution)/shard_map/ppermute | solution.py:407
  71.2 6.1 %collective-permute-start.2 = (f32[16,4,256]{2,1,0:T(4,128)S(1)}, f32[16,4,256]{2,1,0:T(4,128)S(1)}, u32[]{:S(2)}, u32[]{:S(2)}) collective-permute-start(f32[16,4,256]{2,1,0:T(4,128)S(1)} %delta.1.st0_ref), channel_id=1, source_target_pairs={{0,64},{32,96},{64,0},{96,32},{1,65},{33,97},{65,1},{97,33},{2,66}... | collective-permute-start | bytes 196616 | tf_op jit(solution)/shard_map/ppermute | solution.py:407
  71.9 6.1 %collective-permute-start.1 = (f32[16,4,256]{2,1,0:T(4,128)S(1)}, f32[16,4,256]{2,1,0:T(4,128)S(1)}, u32[]{:S(2)}, u32[]{:S(2)}) collective-permute-start(f32[16,4,256]{2,1,0:T(4,128)S(1)} %delta.1.st0_ref), channel_id=1, source_target_pairs={{0,32},{32,64},{64,96},{96,0},{1,33},{33,65},{65,97},{97,1},{2,34}... | collective-permute-start | bytes 196616 | tf_op jit(solution)/shard_map/ppermute | solution.py:407
  78.6 1.0 copy-start.7
  79.5 34.0 %all-to-all-start.2 = ((bf16[64,16,512]{2,1,0:T(8,128)(2,1)}), bf16[64,16,512]{2,1,0:T(8,128)(2,1)S(1)}, u32[]{:S(2)}, u32[]{:S(2)}) async-start(bf16[64,16,512]{2,1,0:T(8,128)(2,1)} %bitcast.20), calls=%async_computation.2 | async-start | bytes 2097152 | tf_op jit(solution)/shard_map/all_to_all | solution.py:409
  87.7 1.6 copy-start.4
  112.6 1.0 copy-start.6
  113.6 1.0 copy-start
  114.6 2.9 %collective-permute-start.4 = (bf16[4,16,16,512]{3,2,1,0:T(8,128)(2,1)}, bf16[4,16,16,512]{3,2,1,0:T(8,128)(2,1)S(1)}, u32[]{:S(2)}, u32[]{:S(2)}) collective-permute-start(bf16[4,16,16,512]{3,2,1,0:T(8,128)(2,1)} %pass_after.1), channel_id=1, source_target_pairs={{0,1},{1,0},{2,3},{3,2},{4,5},{5,4},{6,7},{7,6},{8,9},{9,8},{10,11... | collective-permute-start | bytes 3145736 | tf_op jit(solution)/shard_map/ppermute | solution.py:411
  120.0 10.5 %copy-start.1 = (bf16[64,16,512]{2,1,0:T(8,128)(2,1)S(1)}, bf16[64,16,512]{2,1,0:T(8,128)(2,1)}, u32[]{:S(2)}) copy-start(bf16[64,16,512]{2,1,0:T(8,128)(2,1)} %copy-done) | copy-start | bytes 3145732
  120.0 40.5 %all-to-all-start.3 = ((bf16[64,16,1024]{2,1,0:T(8,128)(2,1)}), bf16[64,16,1024]{2,1,0:T(8,128)(2,1)S(1)}, u32[]{:S(2)}, u32[]{:S(2)}) async-start(bf16[64,16,1024]{2,1,0:T(8,128)(2,1)} %bitcast.11), calls=%async_computation.3 | async-start | bytes 4194304 | tf_op jit(solution)/shard_map/all_to_all | solution.py:412

commit v4 on v3

--- a/solution.py
+++ b/solution.py
@@ -13,7 +13,7 @@
 QT = 16
 KP = 16
 LIST = 160
-WIDE = 1024
+WIDE = 1152
 bf16, f32, i32 = jnp.bfloat16, jnp.float32, jnp.int32
 VMEM = pl.BlockSpec(memory_space=pltpu.VMEM)
 SMEM = pl.BlockSpec(memory_space=pltpu.SMEM)
@@ -30,6 +30,11 @@
 def row_tile(ref, n, first):
     n = jnp.minimum(n, QT - 1)
     return jnp.concatenate([ref[:, n, :, first + h * HD:first + (h + 1) * HD].reshape(64, HD) for h in range(4)], axis=0)
+
+
+def head_tile(refs, n):
+    n = jnp.minimum(n, QT - 1)
+    return jnp.concatenate([ref[:, n].reshape(64, HD) for ref in refs], axis=0)
 
 
 def key_tile(own_ref, oth_ref, p, first):
@@ -122,34 +127,41 @@
         st_ref[n, 1:2, :] = l_s[n]
 
 
-def delta_kernel(st_ref, ot_ref, do_ref, out_ref):
+def delta_kernel(st_ref, ot_ref, do0_ref, do1_ref, do2_ref, do3_ref, out_ref):
+    refs = (do0_ref, do1_ref, do2_ref, do3_ref)
+
     @pl.loop(0, QT, unroll=4)
     def _(n):
-        out_ref[n, 0:2, :] = st_ref[n, 0:2, :]
-        out_ref[n, 2:3, :] = jnp.sum(row_tile(do_ref, n, 0).T.astype(f32) * ot_ref[n], axis=0, keepdims=True)
-
-
-def scale_kernel(st0_ref, st1_ref, st2_ref, st3_ref, ot_ref, stat_ref, out_ref):
+        total = st_ref[n, 1:2, :]
+        some = total > 0.0
+        dots = jnp.sum(head_tile(refs, n).T.astype(f32) * ot_ref[n], axis=0, keepdims=True)
+        out_ref[n, 0:1, :] = jnp.where(some, st_ref[n, 0:1, :] + jnp.log2(total), NEG)
+        out_ref[n, 1:2, :] = jnp.where(some, dots / jnp.where(some, total, 1.0), 0.0)
+
+
+def scale_kernel(st0_ref, st1_ref, st2_ref, st3_ref, st_ref, ot_ref, stat_ref, *out_refs):
     refs = (st0_ref, st1_ref, st2_ref, st3_ref)
 
     @pl.loop(0, QT, unroll=4)
     def _(n):
-        top = refs[0][n, 0:1, :]
-        for ref in refs[1:]:
-            top = jnp.maximum(top, ref[n, 0:1, :])
-        share = [jnp.exp2(ref[n, 0:1, :] - top) for ref in refs]
-        total = sum(w * ref[n, 1:2, :] for w, ref in zip(share, refs))
-        stat_ref[n, 0:1, :] = top + jnp.log2(total)
-        stat_ref[n, 1:2, :] = sum(w * ref[n, 2:3, :] for w, ref in zip(share, refs)) / total
-        ob = (ot_ref[n] * (share[0] / total)).astype(bf16).T
+        parts = [refs[0][n]] + [pltpu.roll(refs[k][n], 64 * k, 1) for k in (1, 2, 3)]
+        top = jnp.maximum(jnp.maximum(parts[0][0:1], parts[1][0:1]), jnp.maximum(parts[2][0:1], parts[3][0:1]))
+        share = [jnp.exp2(part[0:1] - top) for part in parts]
+        total = share[0] + share[1] + share[2] + share[3]
+        lse = top + jnp.log2(total)
+        stat_ref[n, 0:1, :] = lse
+        stat_ref[n, 1:2, :] = sum(w * part[1:2] for w, part in zip(share, parts)) / total
+        ob = (ot_ref[n] * jnp.exp2(st_ref[n, 0:1, :] - lse)).astype(bf16).T
         for h in range(4):
-            out_ref[:, n, :, h * HD:(h + 1) * HD] = ob[h * 64:(h + 1) * 64].reshape(4, 16, HD)
+            out_refs[h][:, n] = ob[h * 64:(h + 1) * 64].reshape(4, 16, HD)
     stat_ref[QT, 0:1, :] = jnp.full((1, 256), -NEG, f32)
     stat_ref[QT, 1:2, :] = jnp.zeros((1, 256), f32)
 
 
-def bwd_kernel(steps, pos_ref, kpos_ref, stat_ref, own_ref, oth_ref, do_ref, out_ref, oth_out_ref,
-               kt, dq, dk, dv, s_buf, dp_buf, p_buf, ds_buf):
+def bwd_kernel(steps, pos_ref, kpos_ref, stat_ref, own_ref, oth_ref, do0_ref, do1_ref, do2_ref, do3_ref, out_ref,
+               oth_out_ref, kt, dq, dk, dv, s_buf, dp_buf, p_buf, ds_buf):
+    do_refs = (do0_ref, do1_ref, do2_ref, do3_ref)
+
     @pl.loop(0, KP, unroll=4)
     def _(p):
         kt[:, pl.ds(pl.multiple_of(p * 256, 256), 256)] = key_tile(own_ref, oth_ref, p, 0).T
@@ -163,7 +175,7 @@
             n, p = unpack(steps, kind, t)
             s = nt(key_tile(own_ref, oth_ref, p, 0), row_tile(own_ref, n, 0)) * SC2
             s_buf[buf] = mask_scores(s, n, p, pos_ref, kpos_ref, NEG) if kind else s
-            dp_buf[buf] = nt(key_tile(own_ref, oth_ref, p, HD), row_tile(do_ref, n, 0))
+            dp_buf[buf] = nt(key_tile(own_ref, oth_ref, p, HD), head_tile(do_refs, n))
 
         def soften(t, buf):
             n, _ = unpack(steps, kind, t)
@@ -174,7 +186,7 @@
         def gather(t, buf):
             n, p = unpack(steps, kind, t)
             ds = ds_buf[buf]
-            dv[p] += nn(p_buf[buf], row_tile(do_ref, n, 0))
+            dv[p] += nn(p_buf[buf], head_tile(do_refs, n))
             dk[p] += nn(ds, row_tile(own_ref, n, 0))
             dq[n] += nn(lanes_at(kt, p), ds)
 
@@ -190,14 +202,14 @@
     def _(n):
         qb = (dq[n] * SCALE).astype(bf16).T
         for h in range(4):
-            out_ref[:, n, :, h * HD:(h + 1) * HD] = qb[h * 64:(h + 1) * 64].reshape(4, 16, HD)
+            out_ref[:, n, :, 640 + h * HD:768 + h * HD] = qb[h * 64:(h + 1) * 64].reshape(4, 16, HD)
 
     @pl.loop(0, KP, unroll=4)
     def _(p):
         for first, tile in ((0, (dk[p] * SCALE).astype(bf16)), (HD, dv[p].astype(bf16))):
             for h in (0, 1):
                 at = 256 * h + first
-                out_ref[:, p, :, 512 + at:512 + at + HD] = tile[64 * h:64 * h + 64].reshape(4, 16, HD)
+                out_ref[:, p, :, at:at + HD] = tile[64 * h:64 * h + 64].reshape(4, 16, HD)
                 oth_out_ref[:, p, :, at:at + HD] = tile[128 + 64 * h:192 + 64 * h].reshape(4, 16, HD)
 
 
@@ -218,25 +230,25 @@
     )(steps, pos, kpos, own, oth)
 
 
-def delta(st, ot, do):
-    return pl.pallas_call(
-        delta_kernel, in_specs=[VMEM] * 3, out_specs=VMEM, out_shape=jax.ShapeDtypeStruct((QT, 4, 256), f32),
+def delta(st, ot, dos):
+    return pl.pallas_call(
+        delta_kernel, in_specs=[VMEM] * 6, out_specs=VMEM, out_shape=jax.ShapeDtypeStruct((QT, 2, 256), f32),
         compiler_params=pltpu.CompilerParams(vmem_limit_bytes=12 << 20), name="delta",
-    )(st, ot, do)
-
-
-def scale(sts, ot):
-    return pl.pallas_call(
-        scale_kernel, in_specs=[VMEM] * 5, out_specs=[VMEM] * 2,
-        out_shape=[jax.ShapeDtypeStruct((QT + 1, 2, 256), f32), jax.ShapeDtypeStruct((4, QT, 16, 512), bf16)],
+    )(st, ot, *dos)
+
+
+def scale(sts, st, ot):
+    return pl.pallas_call(
+        scale_kernel, in_specs=[VMEM] * 6, out_specs=[VMEM] * 5,
+        out_shape=[jax.ShapeDtypeStruct((QT + 1, 2, 256), f32)] + [jax.ShapeDtypeStruct((4, QT, 16, HD), bf16)] * 4,
         compiler_params=pltpu.CompilerParams(vmem_limit_bytes=12 << 20), name="scale",
-    )(*sts, ot)
-
-
-def bwd(steps, pos, kpos, stat, own, oth, do):
+    )(*sts, st, ot)
+
+
+def bwd(steps, pos, kpos, stat, own, oth, dos):
     return pl.pallas_call(
         bwd_kernel,
-        in_specs=[SMEM] + [VMEM] * 6,
+        in_specs=[SMEM] + [VMEM] * 9,
         out_specs=[VMEM] * 2,
         scratch_shapes=[
             pltpu.VMEM((HD, KP * 256), bf16),
@@ -248,12 +260,12 @@
         compiler_params=pltpu.CompilerParams(vmem_limit_bytes=24 << 20),
         cost_estimate=pl.CostEstimate(flops=25 * 10 ** 9, bytes_accessed=8 << 20, transcendentals=0),
         name="bwd",
-    )(steps, pos, kpos, stat, own, oth, do)
-
-
-def pack_kernel(q_hbm, k_hbm, v_hbm, out_hbm, q_ref, k_ref, v_ref, out_ref, in_sem, out_sem):
+    )(steps, pos, kpos, stat, own, oth, *dos)
+
+
+def pack_kernel(q_hbm, k_hbm, v_hbm, do_hbm, out_hbm, q_ref, k_ref, v_ref, do_ref, out_ref, in_sem, out_sem):
     loads = [pltpu.make_async_copy(src, dst, in_sem.at[i])
-             for i, (src, dst) in enumerate(((q_hbm, q_ref), (k_hbm, k_ref), (v_hbm, v_ref)))]
+             for i, (src, dst) in enumerate(((q_hbm, q_ref), (k_hbm, k_ref), (v_hbm, v_ref), (do_hbm, do_ref)))]
     for load in loads:
         load.start()
     for load in loads:
@@ -263,7 +275,12 @@
         for u in range(8):
             for g in range(2):
                 at = u * 2 + g
-                out_ref[j, at, :, 0:512] = q_ref[16 * u:16 * u + 16, 512 * g:512 * g + 512]
+                tokens = slice(16 * u, 16 * u + 16)
+                for r in range(4):
+                    head = 512 * g + HD * ((j - r) % 4)
+                    out_ref[j, at, :, r * HD:r * HD + HD] = q_ref[tokens, head:head + HD]
+                head = 512 * g + HD * j
+                out_ref[j, at, :, 1024:1152] = do_ref[tokens, head:head + HD]
                 for h in (0, 1):
                     rows = slice(32 * j + 16 * h, 32 * j + 16 * h + 16)
                     out_ref[j, at, :, 512 + 256 * h:640 + 256 * h] = k_ref[rows, HD * g:HD * g + HD]
@@ -274,29 +291,15 @@
         store.wait()
 
 
-def pack(q, k, v):
+def pack(q, k, v, do):
     any_spec = pl.BlockSpec(memory_space=pltpu.HBM)
     return pl.pallas_call(
-        pack_kernel, in_specs=[any_spec] * 3, out_specs=any_spec,
+        pack_kernel, in_specs=[any_spec] * 4, out_specs=any_spec,
         out_shape=jax.ShapeDtypeStruct((4, 16, 16, WIDE), bf16),
         scratch_shapes=[pltpu.VMEM((128, 1024), bf16), pltpu.VMEM((128, 256), bf16), pltpu.VMEM((128, 256), bf16),
-                        pltpu.VMEM((4, 16, 16, WIDE), bf16), pltpu.SemaphoreType.DMA((3,)), pltpu.SemaphoreType.DMA((4,))],
+                        pltpu.VMEM((128, 1024), bf16), pltpu.VMEM((4, 16, 16, WIDE), bf16), pltpu.SemaphoreType.DMA((4,)), pltpu.SemaphoreType.DMA((4,))],
         compiler_params=pltpu.CompilerParams(vmem_limit_bytes=60 << 20), name="pack",
-    )(q, k, v)
-
-
-def spread_kernel(do_ref, out_ref):
-    for j in range(4):
-        for u in range(8):
-            for g in range(2):
-                out_ref[j * 16 + u * 2 + g] = do_ref[16 * u:16 * u + 16, 512 * g:512 * g + 512]
-
-
-def spread(do):
-    return pl.pallas_call(
-        spread_kernel, in_specs=[VMEM], out_specs=VMEM, out_shape=jax.ShapeDtypeStruct((64, 16, 512), bf16),
-        compiler_params=pltpu.CompilerParams(vmem_limit_bytes=12 << 20), name="spread",
-    )(do)
+    )(q, k, v, do)
 
 
 def pass_kernel(*refs):
@@ -306,54 +309,50 @@
 def pass_after(x, earlier):
     any_spec = pl.BlockSpec(memory_space=pl.ANY)
     return pl.pallas_call(
-        pass_kernel, in_specs=[any_spec] * 2, out_specs=any_spec, out_shape=jax.ShapeDtypeStruct(x.shape, x.dtype),
-        input_output_aliases={0: 0}, name="pass_after",
-    )(x, earlier)
-
-
-def add_kernel(own_ref, other_ref, out_ref):
-    out_ref[...] = (own_ref[...].astype(f32) + other_ref[...].astype(f32)).astype(bf16)
-
-
-def add_other(out, other):
-    last = pl.BlockSpec((4, KP, 16, 512), lambda i: (0, 0, 0, 1))
-    return pl.pallas_call(
-        add_kernel, grid=(1,), in_specs=[last, pl.BlockSpec((4, KP, 16, 512), lambda i: (0, 0, 0, 0))], out_specs=last,
+        pass_kernel, in_specs=[any_spec] * (1 + len(earlier)), out_specs=any_spec,
+        out_shape=jax.ShapeDtypeStruct(x.shape, x.dtype), input_output_aliases={0: 0}, name="pass_after",
+    )(x, *earlier)
+
+
+def add_kernel(own_ref, other_ref, o0_ref, o1_ref, o2_ref, o3_ref, out_ref):
+    out_ref[..., :512] = (own_ref[..., :512].astype(f32) + other_ref[...].astype(f32)).astype(bf16)
+    total = o0_ref[...].astype(f32) + o1_ref[...].astype(f32) + o2_ref[...].astype(f32) + o3_ref[...].astype(f32)
+    out_ref[..., 512:] = total.astype(bf16)
+
+
+def add_parts(out, other, heads):
+    block = lambda columns: pl.BlockSpec((1, KP, 16, columns), lambda i: (i, 0, 0, 0))
+    return pl.pallas_call(
+        add_kernel, grid=(4,), in_specs=[block(640), block(512)] + [block(HD)] * 4, out_specs=block(640),
         out_shape=jax.ShapeDtypeStruct(out.shape, bf16), input_output_aliases={0: 0},
-        compiler_params=pltpu.CompilerParams(vmem_limit_bytes=12 << 20), name="add_cores",
-    )(out, other)
-
-
-def sum_rows(in_ref, out_ref):
+        compiler_params=pltpu.CompilerParams(vmem_limit_bytes=12 << 20), name="add_parts",
+    )(out, other, *heads)
+
+
+def sum_kernel(in_ref, at_ref, qg_ref, kg_ref, vg_ref):
     for u in range(8):
         for g in range(2):
-            parts = [in_ref[j * 16 + u * 2 + g, :, 0:512].astype(f32) for j in range(4)]
-            out_ref[16 * u:16 * u + 16, 512 * g:512 * g + 512] = (parts[0] + parts[1] + parts[2] + parts[3]).astype(bf16)
-
-
-def sum_attended(pieces):
-    return pl.pallas_call(
-        sum_rows, in_specs=[VMEM], out_specs=VMEM, out_shape=jax.ShapeDtypeStruct((128, 1024), bf16),
-        compiler_params=pltpu.CompilerParams(vmem_limit_bytes=12 << 20), name="sum_attended",
-    )(pieces)
-
-
-def sum_kernel(in_ref, qg_ref, kg_ref, vg_ref):
-    sum_rows(in_ref, qg_ref)
+            rows = slice(16 * u, 16 * u + 16)
+            for h in range(4):
+                cols = slice(512 * g + HD * h, 512 * g + HD * h + HD)
+                at_ref[rows, cols] = in_ref[h * 16 + u * 2 + g, :, 512:640]
+                first = [640 + HD * ((j - h) % 4) for j in range(4)]
+                parts = [in_ref[j * 16 + u * 2 + g, :, first[j]:first[j] + HD].astype(f32) for j in range(4)]
+                qg_ref[rows, cols] = (parts[0] + parts[1] + parts[2] + parts[3]).astype(bf16)
     for j in range(4):
         for g in range(2):
             for h in (0, 1):
                 rows, cols = slice(32 * j + 16 * h, 32 * j + 16 * h + 16), slice(HD * g, HD * g + HD)
-                both = sum(in_ref[j * 16 + u * 2 + g, :, 512 + 256 * h:768 + 256 * h].astype(f32) for u in range(8))
+                both = sum(in_ref[j * 16 + u * 2 + g, :, 256 * h:256 * h + 256].astype(f32) for u in range(8))
                 kg_ref[rows, cols] = both[:, :HD].astype(bf16)
                 vg_ref[rows, cols] = both[:, HD:].astype(bf16)
 
 
-def sum_grads(pieces):
+def sum_pieces(pieces):
     big, small = jax.ShapeDtypeStruct((128, 1024), bf16), jax.ShapeDtypeStruct((128, 256), bf16)
     return pl.pallas_call(
-        sum_kernel, in_specs=[VMEM], out_specs=[VMEM] * 3, out_shape=[big, small, small],
-        compiler_params=pltpu.CompilerParams(vmem_limit_bytes=12 << 20), name="sum_grads",
+        sum_kernel, in_specs=[VMEM], out_specs=[VMEM] * 4, out_shape=[big, big, small, small],
+        compiler_params=pltpu.CompilerParams(vmem_limit_bytes=12 << 20), name="sum_pieces",
     )(pieces)
 
 
@@ -397,21 +396,25 @@
     j, u, core = (lax.axis_index(name) for name in ("head", "inner", "core"))
     swap = [(0, 1), (1, 0)]
     steps, pos, kpos = make_plan(lengths, core, u, j)
-    pieces = pack(query_rows.reshape(128, 1024), key_rows.reshape(128, 256), value_rows.reshape(128, 256))
-    own = lax.all_to_all(pieces.reshape(64, 16, WIDE), PLANE, 0, 0, tiled=True)
-    own = own.reshape(4, QT, 16, WIDE)
-    do = lax.all_to_all(spread(out_grad.reshape(128, 1024)), PLANE, 0, 0, tiled=True).reshape(4, QT, 16, 512)
-    oth = lax.ppermute(own[..., 512:], "core", swap)
+    pieces = pack(query_rows.reshape(128, 1024), key_rows.reshape(128, 256), value_rows.reshape(128, 256),
+                  out_grad.reshape(128, 1024))
+    own = lax.all_to_all(pieces.reshape(64, 16, WIDE), PLANE, 0, 0, tiled=True).reshape(4, QT, 16, WIDE)
+    oth = lax.ppermute(own[..., 512:1024], "core", swap)
+
+    def along(x, k):
+        return lax.ppermute(x, "head", [(i, (i + k) % 4) for i in range(4)])
+
+    do = own[..., 1024:]
+    dos = [do] + [along(do, k) for k in (1, 2, 3)]
     ot, st = fwd(steps, pos, kpos, own, oth)
-    st = delta(st, ot, do)
-    sts = [st] + [lax.ppermute(st, "head", [(i, (i + k) % 4) for i in range(4)]) for k in (1, 2, 3)]
-    stat, scaled = scale(sts, ot)
-    scaled = lax.all_to_all(scaled.reshape(64, 16, 512), PLANE, 0, 0, tiled=True)
-    out, oth_out = bwd(steps, pos, kpos, stat, own, oth, do)
-    out = add_other(out, lax.ppermute(pass_after(oth_out, scaled), "core", swap))
+    part = delta(st, ot, dos)
+    stat, *heads = scale([part] + [along(part, k) for k in (1, 2, 3)], st, ot)
+    heads = heads[:1] + [along(heads[k], -k) for k in (1, 2, 3)]
+    out, oth_out = bwd(steps, pos, kpos, stat, own, oth, dos)
+    oth_out = pass_after(oth_out, heads[1:])
+    out = add_parts(out, lax.ppermute(oth_out, "core", swap), heads)
     out = lax.all_to_all(out.reshape(64, 16, WIDE), PLANE, 0, 0, tiled=True)
-    attended = sum_attended(scaled)
-    query_grad, key_grad, value_grad = sum_grads(out)
+    attended, query_grad, key_grad, value_grad = sum_pieces(out)
     return (attended.reshape(1, 1, 128, 1024), query_grad.reshape(1, 1, 128, 1024),
             key_grad.reshape(1, 1, 128, 256), value_grad.reshape(1, 1, 128, 256))
 

time: 162 us -> 150 us (0.926)
  blocking collectives: 0 us -> 40.8 us
  waiting for transfers between devices: 65 us -> 40 us
  starting transfers between devices: 40 us -> 19.7 us
  Pallas kernels: 43.2 us -> 38.8 us
  local copies, waits for them, and re-layouts: 9.19 us -> 6.91 us
    all_to_all x0 -> x1, blocking collectives: none -> 40.8 us  [on_device(): out = lax.all_to_all(out.reshape(64, 16, WIDE), PLANE, 0, 0, tiled=True)]
    all_to_all x4 -> x1, waiting for transfers between devices: 56.3 us -> 30.7 us  [on_device(): lax.all_to_all(pieces.reshape(64, 16, WIDE), PLANE, 0, 0, tiled=True)]
    all_to_all x4 -> x1, starting transfers between devices: 35.6 us -> 11.5 us  [on_device(): lax.all_to_all(pieces.reshape(64, 16, WIDE), PLANE, 0, 0, tiled=True)]
    pallas_call x9 -> x7, Pallas kernels: 31.1 us -> 27.1 us  [the longest x1 21.2 us: bwd(): pl.pallas_call(bwd_kernel, in_specs=[SMEM] + [VMEM] * 9, out_specs=[VMEM]...]
    ppermute x5 -> x11, starting transfers between devices: 4.48 us -> 8.18 us  [the longest x9 8.17 us: along(): return lax.ppermute(x, 'head', [(i, (i + k) % 4) for i in range(4)])]
    unnamed x20 -> x24, local copies, waits for them, and re-layouts: 7.11 us -> 4.67 us
    ppermute x5 -> x11, waiting for transfers between devices: 8.68 us -> 9.3 us  [the longest x9 6.43 us: along(): return lax.ppermute(x, 'head', [(i, (i + k) % 4) for i in range(4)])]
  transfers between devices with their start and end apart: 9 -> 12, of which waited for: 8 -> 6; matrix products, arithmetic and copies ran while one was open for 3% -> 3% of each run, Pallas kernels for 22% -> 22%
where the time goes in v4:
time: 150 us
  blocking collectives  40.8 us (27%)
  waiting for transfers between devices  40 us (27%)
  Pallas kernels  38.8 us (26%)
  starting transfers between devices  19.7 us (13%)
  local copies, waits for them, and re-layouts  6.91 us (5%)
  other arithmetic  2.98 us (2%)
    all_to_all x1, blocking collectives, on_device(): out = lax.all_to_all(out.reshape(64, 16, WIDE), PLANE, 0, 0, tiled=True)  40.8 us
    all_to_all x1, waiting for transfers between devices, on_device(): lax.all_to_all(pieces.reshape(64, 16, WIDE), PLANE, 0, 0, tiled=True)  30.7 us
    pallas_call x1, Pallas kernels, bwd(): pl.pallas_call(bwd_kernel, in_specs=[SMEM] + [VMEM] * 9, out_specs=[VMEM]...  21.2 us
    pallas_call x1, Pallas kernels, fwd(): pl.pallas_call(fwd_kernel, in_specs=[SMEM] + [VMEM] * 4, out_specs=[VMEM,...  11.7 us
    all_to_all x1, starting transfers between devices, on_device(): lax.all_to_all(pieces.reshape(64, 16, WIDE), PLANE, 0, 0, tiled=True)  11.5 us
    ppermute x9, starting transfers between devices, along(): return lax.ppermute(x, 'head', [(i, (i + k) % 4) for i in range(4)])  8.17 us
    ppermute x9, waiting for transfers between devices, along(): return lax.ppermute(x, 'head', [(i, (i + k) % 4) for i in range(4)])  6.43 us
    unnamed x24, local copies, waits for them, and re-layouts  4.67 us
  transfers between devices with their start and end apart: 12, of which 6 were waited for; matrix products, arithmetic and copies ran while one was open for 3% of the time, Pallas kernels for 22%

profile of v4, /device:TPU:0, one launch (start us, length us, event | category | flops | bytes accessed | tf_op | source)
XLA Modules:
  0.0 150.1 jit_solution(18365068434255734344)
XLA Ops:
  0.6 2.7 %pack.1 = bf16[4,16,16,1152]{3,2,1,0:T(8,128)(2,1)} custom-call(bf16[128,1024]{1,0:T(8,128)(2,1)} %bitcast.19, bf16[128,256]{1,0:T(8,128)(2,1)} %bitcast.21, bf16[128,256]{1,0:T(8,128)(2,1)} %bitcast.22, bf16[128,1024]{1,0:T(8,128)(2,1)} %bitcast.20), custom_call_target="tpu_custom_call" | custom-call | tf_op jit(solution)/shard_map/pack/pallas_call | solution.py:296
  3.3 0.0 copy-start.11
  3.3 11.5 %all-to-all-start = ((bf16[64,16,1152]{2,1,0:T(8,128)(2,1)}), bf16[64,16,1152]{2,1,0:T(8,128)(2,1)S(1)}, u32[]{:S(2)}, u32[]{:S(2)}) async-start(bf16[64,16,1152]{2,1,0:T(8,128)(2,1)} %bitcast.18), calls=%async_computation | async-start | bytes 4718592 | tf_op jit(solution)/shard_map/all_to_all | solution.py:401
  14.9 0.1 and.222
  15.0 0.1 and.227
  15.1 0.1 add.207
  15.2 0.1 sub.124
  15.2 0.1 add_add_fusion
  15.3 0.1 add.204
  15.4 0.1 add.205
  15.5 0.0 copy-done.11
  15.5 0.1 select_reduce_fusion.3
  15.6 0.1 select_reduce_fusion.2
  15.7 0.2 fusion.4
  15.9 0.1 ge.95
  16.0 0.1 and.226
  16.1 0.1 convert_reduce_fusion
  16.2 0.1 convert_reduce_fusion.1
  16.4 0.2 select_reduce_fusion.1
  16.5 30.7 %all-to-all-done = bf16[64,16,1152]{2,1,0:T(8,128)(2,1)S(1)} async-done(((bf16[64,16,1152]{2,1,0:T(8,128)(2,1)}), bf16[64,16,1152]{2,1,0:T(8,128)(2,1)S(1)}, u32[]{:S(2)}, u32[]{:S(2)}) %all-to-all-start) | async-done | bytes 2359328 | tf_op jit(solution)/shard_map/all_to_all | solution.py:401
  47.2 1.2 slice.18
  48.5 0.0 collective-permute-start
  48.5 0.1 tile.18
  48.6 0.1 tile.16
  48.7 0.7 convert_reduce_fusion.3
  49.4 0.6 compare_select_fusion.1
  50.1 0.7 compare_select_fusion
  50.8 1.2 collective-permute-start.3
  52.0 1.0 collective-permute-start.2
  53.0 0.5 collective-permute-start.1
  53.5 0.0 collective-permute-done.oth_ref
  53.5 0.1 broadcast_in_dim.85.kpos_ref
  53.6 11.7 %fwd.1 = (f32[16,128,256]{2,1,0:T(8,128)S(1)}, f32[16,4,256]{2,1,0:T(4,128)S(1)}) custom-call(s32[2,160]{1,0:T(2,128)S(1)} %pad_add_fusion.1.steps, s32[17,2,256]{2,1,0:T(2,128)S(1)} %pad_add_fusion.pos_ref, s32[256,128]{1,0:T(8,128)S(1)} %broadcast_in_dim.85.kpos_ref, bf16[4,16,16,1152]{3,2,1,0:T(8,128)(2,1)S(1)} %bitcast.16, ...), custom_call_target="tpu_custom_call" | custom-call | flops 15000000512 | bytes 8388608 | tf_op jit(solution)/shard_map/fwd/pallas_call | solution.py:217
  65.3 0.0 collective-permute-done.3.do3_ref
  65.3 0.0 collective-permute-done.2.do2_ref
  65.3 2.2 %collective-permute-done.1.do1_ref = bf16[4,16,16,128]{3,2,1,0:T(8,128)(2,1)S(1)} collective-permute-done((bf16[4,16,16,128]{3,2,1,0:T(8,128)(2,1)S(1)}, bf16[4,16,16,128]{3,2,1,0:T(8,128)(2,1)S(1)}, u32[]{:S(2)}, u32[]{:S(2)}) %collective-permute-start.1) | collective-permute-done | bytes 262176 | tf_op jit(solution)/shard_map/ppermute | solution.py:405
  67.6 0.6 delta.1.st0_ref
  68.1 0.7 collective-permute-start.6
  68.8 1.3 collective-permute-start.5
  70.1 0.9 collective-permute-start.4
  71.0 1.1 collective-permute-done.6.st3_ref
  72.1 2.1 %collective-permute-done.5.st2_ref = f32[16,2,256]{2,1,0:T(2,128)S(1)} collective-permute-done((f32[16,2,256]{2,1,0:T(2,128)S(1)}, f32[16,2,256]{2,1,0:T(2,128)S(1)}, u32[]{:S(2)}, u32[]{:S(2)}) %collective-permute-start.5) | collective-permute-done | bytes 32800 | tf_op jit(solution)/shard_map/ppermute | solution.py:405
  74.2 1.0 collective-permute-done.4.st1_ref
  75.2 1.0 scale.1
  76.2 1.7 %collective-permute-start.7 = (bf16[4,16,16,128]{3,2,1,0:T(8,128)(2,1)S(1)}, bf16[4,16,16,128]{3,2,1,0:T(8,128)(2,1)S(1)}, u32[]{:S(2)}, u32[]{:S(2)}) collective-permute-start(bf16[4,16,16,128]{3,2,1,0:T(8,128)(2,1)S(1)} %get-tuple-element.22), channel_id=1, source_target_pairs={{0,96},{32,0},{64,32},{96,64},{1,97},{33,1},{65,33},{97,65},{2,98}... | collective-permute-start | bytes 786440 | tf_op jit(solution)/shard_map/ppermute | solution.py:405
  77.9 0.9 collective-permute-start.8
  78.8 0.0 collective-permute-start.9
  78.8 21.2 %bwd.1 = (bf16[4,16,16,1152]{3,2,1,0:T(8,128)(2,1)S(1)}, bf16[4,16,16,512]{3,2,1,0:T(8,128)(2,1)S(1)}) custom-call(s32[2,160]{1,0:T(2,128)S(1)} %pad_add_fusion.1.steps, s32[17,2,256]{2,1,0:T(2,128)S(1)} %pad_add_fusion.pos_ref, s32[256,128]{1,0:T(8,128)S(1)} %broadcast_in_dim.85.kpos_ref, f32[17,2,256]{2,1,0:T(2,128)S(1)} %get-tuple-element.19.stat_ref, ...), custom_call_target="tpu_custom_call" | custom-call | flops 24999999488 | bytes 8388608 | tf_op jit(solution)/shard_map/bwd/pallas_call | solution.py:249
  100.1 1.0 copy-done.2
  101.0 0.0 collective-permute-done.7.refs_1_.o1_ref
  101.0 0.0 collective-permute-done.8.refs_2_.o2_ref
  101.0 0.0 copy-start.5
  101.1 0.0 collective-permute-done.9.refs_3_.o3_ref
  101.1 0.7 copy-done.3
  101.7 0.1 copy-done.5
  101.8 0.1 copy-done.7
  101.9 0.0 collective-permute-start.10
  101.9 2.9 %collective-permute-done.10.other_ref = bf16[4,16,16,512]{3,2,1,0:T(8,128)(2,1)S(1)} collective-permute-done((bf16[4,16,16,512]{3,2,1,0:T(8,128)(2,1)}, bf16[4,16,16,512]{3,2,1,0:T(8,128)(2,1)S(1)}, u32[]{:S(2)}, u32[]{:S(2)}) %collective-permute-start.10) | collective-permute-done | bytes 1048608 | tf_op jit(solution)/shard_map/ppermute | solution.py:415
  104.8 0.9 copy-done.4
  105.7 0.9 copy-done.6
  106.7 0.9 copy-done.8
  107.6 0.7 add_parts.1
  108.3 40.8 %all_to_all.10.in_ref = bf16[64,16,1152]{2,1,0:T(8,128)(2,1)S(1)} all-to-all(bf16[64,16,1152]{2,1,0:T(8,128)(2,1)S(1)} %bitcast.13), channel_id=1, replica_groups=mesh['head'=4,'inner'=8,'zl'=2,'core'=2] {'head','inner','zl'}, dimensions={0} | all-to-all | bytes 4718592 | tf_op jit(solution)/shard_map/all_to_all | solution.py:416
  149.1 1.0 sum_pieces.1
  (34 shorter events, 0.2 us)
Async XLA Ops:
  3.3 12.2 %copy-start.11 = (s32[4]{0:T(128)S(1)}, s32[4]{0:T(128)}, u32[]{:S(2)}) copy-start(s32[4]{0:T(128)} %param.9) | copy-start | bytes 52
  3.3 43.9 %all-to-all-start = ((bf16[64,16,1152]{2,1,0:T(8,128)(2,1)}), bf16[64,16,1152]{2,1,0:T(8,128)(2,1)S(1)}, u32[]{:S(2)}, u32[]{:S(2)}) async-start(bf16[64,16,1152]{2,1,0:T(8,128)(2,1)} %bitcast.18), calls=%async_computation | async-start | bytes 4718592 | tf_op jit(solution)/shard_map/all_to_all | solution.py:401
  47.2 18.1 %copy-start = (bf16[64,16,1152]{2,1,0:T(8,128)(2,1)}, bf16[64,16,1152]{2,1,0:T(8,128)(2,1)S(1)}, u32[]{:S(2)}) copy-start(bf16[64,16,1152]{2,1,0:T(8,128)(2,1)S(1)} %all-to-all-done) | copy-start | bytes 7077892
  48.5 5.1 %collective-permute-start = (bf16[4,16,16,512]{3,2,1,0:T(8,128)(2,1)}, bf16[4,16,16,512]{3,2,1,0:T(8,128)(2,1)S(1)}, u32[]{:S(2)}, u32[]{:S(2)}) collective-permute-start(bf16[4,16,16,512]{3,2,1,0:T(8,128)(2,1)} %slice.18), channel_id=1, source_target_pairs={{0,1},{1,0},{2,3},{3,2},{4,5},{5,4},{6,7},{7,6},{8,9},{9,8},{10,11... | collective-permute-start | bytes 3145736 | tf_op jit(solution)/shard_map/ppermute | solution.py:402
  50.8 14.5 %collective-permute-start.3 = (bf16[4,16,16,128]{3,2,1,0:T(8,128)(2,1)S(1)}, bf16[4,16,16,128]{3,2,1,0:T(8,128)(2,1)S(1)}, u32[]{:S(2)}, u32[]{:S(2)}) collective-permute-start(bf16[4,16,16,128]{3,2,1,0:T(8,128)(2,1)S(1)} %slice.19.do0_ref), channel_id=1, source_target_pairs={{0,96},{32,0},{64,32},{96,64},{1,97},{33,1},{65,33},{97,65},{2,98}... | collective-permute-start | bytes 786440 | tf_op jit(solution)/shard_map/ppermute | solution.py:405
  52.0 13.3 %collective-permute-start.2 = (bf16[4,16,16,128]{3,2,1,0:T(8,128)(2,1)S(1)}, bf16[4,16,16,128]{3,2,1,0:T(8,128)(2,1)S(1)}, u32[]{:S(2)}, u32[]{:S(2)}) collective-permute-start(bf16[4,16,16,128]{3,2,1,0:T(8,128)(2,1)S(1)} %slice.19.do0_ref), channel_id=1, source_target_pairs={{0,64},{32,96},{64,0},{96,32},{1,65},{33,97},{65,1},{97,33},{2,66}... | collective-permute-start | bytes 786440 | tf_op jit(solution)/shard_map/ppermute | solution.py:405
  53.0 14.6 %collective-permute-start.1 = (bf16[4,16,16,128]{3,2,1,0:T(8,128)(2,1)S(1)}, bf16[4,16,16,128]{3,2,1,0:T(8,128)(2,1)S(1)}, u32[]{:S(2)}, u32[]{:S(2)}) collective-permute-start(bf16[4,16,16,128]{3,2,1,0:T(8,128)(2,1)S(1)} %slice.19.do0_ref), channel_id=1, source_target_pairs={{0,32},{32,64},{64,96},{96,0},{1,33},{33,65},{65,97},{97,1},{2,34}... | collective-permute-start | bytes 786440 | tf_op jit(solution)/shard_map/ppermute | solution.py:405
  53.5 11.8 %copy-start.9 = (bf16[4,16,16,512]{3,2,1,0:T(8,128)(2,1)}, bf16[4,16,16,512]{3,2,1,0:T(8,128)(2,1)S(1)}, u32[]{:S(2)}) copy-start(bf16[4,16,16,512]{3,2,1,0:T(8,128)(2,1)S(1)} %collective-permute-done.oth_ref) | copy-start | bytes 3145732
  67.6 11.3 %copy-start.1 = (bf16[64,16,1152]{2,1,0:T(8,128)(2,1)S(1)}, bf16[64,16,1152]{2,1,0:T(8,128)(2,1)}, u32[]{:S(2)}) copy-start(bf16[64,16,1152]{2,1,0:T(8,128)(2,1)} %copy-done) | copy-start | bytes 7077892
  67.6 11.3 %copy-start.10 = (bf16[4,16,16,512]{3,2,1,0:T(8,128)(2,1)S(1)}, bf16[4,16,16,512]{3,2,1,0:T(8,128)(2,1)}, u32[]{:S(2)}) copy-start(bf16[4,16,16,512]{3,2,1,0:T(8,128)(2,1)} %copy-done.9) | copy-start | bytes 3145732
  68.1 4.0 %collective-permute-start.6 = (f32[16,2,256]{2,1,0:T(2,128)S(1)}, f32[16,2,256]{2,1,0:T(2,128)S(1)}, u32[]{:S(2)}, u32[]{:S(2)}) collective-permute-start(f32[16,2,256]{2,1,0:T(2,128)S(1)} %delta.1.st0_ref), channel_id=1, source_target_pairs={{0,96},{32,0},{64,32},{96,64},{1,97},{33,1},{65,33},{97,65},{2,98}... | collective-permute-start | bytes 98312 | tf_op jit(solution)/shard_map/ppermute | solution.py:405
  68.8 5.4 %collective-permute-start.5 = (f32[16,2,256]{2,1,0:T(2,128)S(1)}, f32[16,2,256]{2,1,0:T(2,128)S(1)}, u32[]{:S(2)}, u32[]{:S(2)}) collective-permute-start(f32[16,2,256]{2,1,0:T(2,128)S(1)} %delta.1.st0_ref), channel_id=1, source_target_pairs={{0,64},{32,96},{64,0},{96,32},{1,65},{33,97},{65,1},{97,33},{2,66}... | collective-permute-start | bytes 98312 | tf_op jit(solution)/shard_map/ppermute | solution.py:405
  70.1 5.1 %collective-permute-start.4 = (f32[16,2,256]{2,1,0:T(2,128)S(1)}, f32[16,2,256]{2,1,0:T(2,128)S(1)}, u32[]{:S(2)}, u32[]{:S(2)}) collective-permute-start(f32[16,2,256]{2,1,0:T(2,128)S(1)} %delta.1.st0_ref), channel_id=1, source_target_pairs={{0,32},{32,64},{64,96},{96,0},{1,33},{33,65},{65,97},{97,1},{2,34}... | collective-permute-start | bytes 98312 | tf_op jit(solution)/shard_map/ppermute | solution.py:405
  76.2 24.8 %collective-permute-start.7 = (bf16[4,16,16,128]{3,2,1,0:T(8,128)(2,1)S(1)}, bf16[4,16,16,128]{3,2,1,0:T(8,128)(2,1)S(1)}, u32[]{:S(2)}, u32[]{:S(2)}) collective-permute-start(bf16[4,16,16,128]{3,2,1,0:T(8,128)(2,1)S(1)} %get-tuple-element.22), channel_id=1, source_target_pairs={{0,96},{32,0},{64,32},{96,64},{1,97},{33,1},{65,33},{97,65},{2,98}... | collective-permute-start | bytes 786440 | tf_op jit(solution)/shard_map/ppermute | solution.py:405
  77.9 23.2 %collective-permute-start.8 = (bf16[4,16,16,128]{3,2,1,0:T(8,128)(2,1)S(1)}, bf16[4,16,16,128]{3,2,1,0:T(8,128)(2,1)S(1)}, u32[]{:S(2)}, u32[]{:S(2)}) collective-permute-start(bf16[4,16,16,128]{3,2,1,0:T(8,128)(2,1)S(1)} %get-tuple-element.23), channel_id=1, source_target_pairs={{0,64},{32,96},{64,0},{96,32},{1,65},{33,97},{65,1},{97,33},{2,66}... | collective-permute-start | bytes 786440 | tf_op jit(solution)/shard_map/ppermute | solution.py:405
  78.8 22.3 %collective-permute-start.9 = (bf16[4,16,16,128]{3,2,1,0:T(8,128)(2,1)S(1)}, bf16[4,16,16,128]{3,2,1,0:T(8,128)(2,1)S(1)}, u32[]{:S(2)}, u32[]{:S(2)}) collective-permute-start(bf16[4,16,16,128]{3,2,1,0:T(8,128)(2,1)S(1)} %get-tuple-element.24), channel_id=1, source_target_pairs={{0,32},{32,64},{64,96},{96,0},{1,33},{33,65},{65,97},{97,1},{2,34}... | collective-permute-start | bytes 786440 | tf_op jit(solution)/shard_map/ppermute | solution.py:405
  100.1 1.0 copy-start.2
  101.0 0.7 copy-start.3
  101.0 0.8 copy-start.5
  101.1 0.8 copy-start.7
  101.9 2.9 %collective-permute-start.10 = (bf16[4,16,16,512]{3,2,1,0:T(8,128)(2,1)}, bf16[4,16,16,512]{3,2,1,0:T(8,128)(2,1)S(1)}, u32[]{:S(2)}, u32[]{:S(2)}) collective-permute-start(bf16[4,16,16,512]{3,2,1,0:T(8,128)(2,1)} %pass_after.1), channel_id=1, source_target_pairs={{0,1},{1,0},{2,3},{3,2},{4,5},{5,4},{6,7},{7,6},{8,9},{9,8},{10,11... | collective-permute-start | bytes 3145736 | tf_op jit(solution)/shard_map/ppermute | solution.py:415
  104.8 1.0 copy-start.4
  105.7 0.9 copy-start.6
  106.7 0.9 copy-start.8

commit v5 on v4

--- a/solution.py
+++ b/solution.py
@@ -302,31 +302,32 @@
     )(q, k, v, do)
 
 
-def pass_kernel(*refs):
-    del refs
-
-
-def pass_after(x, earlier):
-    any_spec = pl.BlockSpec(memory_space=pl.ANY)
-    return pl.pallas_call(
-        pass_kernel, in_specs=[any_spec] * (1 + len(earlier)), out_specs=any_spec,
-        out_shape=jax.ShapeDtypeStruct(x.shape, x.dtype), input_output_aliases={0: 0}, name="pass_after",
-    )(x, *earlier)
-
-
-def add_kernel(own_ref, other_ref, o0_ref, o1_ref, o2_ref, o3_ref, out_ref):
+def gather_kernel(oth_ref, o0_ref, o1_ref, o2_ref, o3_ref, out_ref, sum_ref):
+    out_ref[...] = oth_ref[...]
+    total = o0_ref[...].astype(f32) + o1_ref[...].astype(f32) + o2_ref[...].astype(f32) + o3_ref[...].astype(f32)
+    sum_ref[...] = total.astype(bf16)
+
+
+def gather_parts(oth, heads):
+    return pl.pallas_call(
+        gather_kernel, in_specs=[VMEM] * 5, out_specs=[VMEM] * 2,
+        out_shape=[jax.ShapeDtypeStruct(oth.shape, bf16), jax.ShapeDtypeStruct(heads[0].shape, bf16)],
+        compiler_params=pltpu.CompilerParams(vmem_limit_bytes=12 << 20), name="gather_parts",
+    )(oth, *heads)
+
+
+def add_kernel(own_ref, other_ref, head_ref, out_ref):
     out_ref[..., :512] = (own_ref[..., :512].astype(f32) + other_ref[...].astype(f32)).astype(bf16)
-    total = o0_ref[...].astype(f32) + o1_ref[...].astype(f32) + o2_ref[...].astype(f32) + o3_ref[...].astype(f32)
-    out_ref[..., 512:] = total.astype(bf16)
-
-
-def add_parts(out, other, heads):
+    out_ref[..., 512:] = head_ref[...]
+
+
+def add_parts(out, other, head):
     block = lambda columns: pl.BlockSpec((1, KP, 16, columns), lambda i: (i, 0, 0, 0))
     return pl.pallas_call(
-        add_kernel, grid=(4,), in_specs=[block(640), block(512)] + [block(HD)] * 4, out_specs=block(640),
+        add_kernel, grid=(4,), in_specs=[block(640), block(512), block(HD)], out_specs=block(640),
         out_shape=jax.ShapeDtypeStruct(out.shape, bf16), input_output_aliases={0: 0},
         compiler_params=pltpu.CompilerParams(vmem_limit_bytes=12 << 20), name="add_parts",
-    )(out, other, *heads)
+    )(out, other, head)
 
 
 def sum_kernel(in_ref, at_ref, qg_ref, kg_ref, vg_ref):
@@ -411,8 +412,8 @@
     stat, *heads = scale([part] + [along(part, k) for k in (1, 2, 3)], st, ot)
     heads = heads[:1] + [along(heads[k], -k) for k in (1, 2, 3)]
     out, oth_out = bwd(steps, pos, kpos, stat, own, oth, dos)
-    oth_out = pass_after(oth_out, heads[1:])
-    out = add_parts(out, lax.ppermute(oth_out, "core", swap), heads)
+    oth_out, head = gather_parts(oth_out, heads)
+    out = add_parts(out, lax.ppermute(oth_out, "core", swap), head)
     out = lax.all_to_all(out.reshape(64, 16, WIDE), PLANE, 0, 0, tiled=True)
     attended, query_grad, key_grad, value_grad = sum_pieces(out)
     return (attended.reshape(1, 1, 128, 1024), query_grad.reshape(1, 1, 128, 1024),

time: 150 us -> 148 us (0.987); the launches traced: 150 us -> 150 us
  Pallas kernels: 38.8 us -> 43.6 us
  local copies, waits for them, and re-layouts: 6.91 us -> 2.16 us
  waiting for transfers between devices: 40 us -> 37.7 us
  starting transfers between devices: 19.7 us -> 21.6 us
    unnamed x24 -> x2, local copies, waits for them, and re-layouts: 4.67 us -> 0.01 us
    pallas_call x1, Pallas kernels: 21.2 us -> 23.9 us  [bwd(): pl.pallas_call(bwd_kernel, in_specs=[SMEM] + [VMEM] * 9, out_specs=[VMEM]...]
    pallas_call x1, Pallas kernels: 11.7 us -> 13.7 us  [fwd(): pl.pallas_call(fwd_kernel, in_specs=[SMEM] + [VMEM] * 4, out_specs=[VMEM,...]
    ppermute x9, waiting for transfers between devices: 6.43 us -> 4.39 us  [along(): return lax.ppermute(x, 'head', [(i, (i + k) % 4) for i in range(4)])]
    ppermute x9, starting transfers between devices: 8.17 us -> 9.99 us  [along(): return lax.ppermute(x, 'head', [(i, (i + k) % 4) for i in range(4)])]
  transfers between devices with their start and end apart: 12 -> 12, of which waited for: 6 -> 5; matrix products, arithmetic and copies ran while one was open for 3% -> 3% of each run, Pallas kernels for 22% -> 25%
where the time goes in v5:
time: 148 us; the launch traced here: 150 us
  Pallas kernels  43.6 us (29%)
  blocking collectives  41 us (28%)
  waiting for transfers between devices  37.7 us (25%)
  starting transfers between devices  21.6 us (15%)
  other arithmetic  2.98 us (2%)
  local copies, waits for them, and re-layouts  2.16 us (1%)
    all_to_all x1, blocking collectives, on_device(): out = lax.all_to_all(out.reshape(64, 16, WIDE), PLANE, 0, 0, tiled=True)  41 us
    all_to_all x1, waiting for transfers between devices, on_device(): lax.all_to_all(pieces.reshape(64, 16, WIDE), PLANE, 0, 0, tiled=True)  30.7 us
    pallas_call x1, Pallas kernels, bwd(): pl.pallas_call(bwd_kernel, in_specs=[SMEM] + [VMEM] * 9, out_specs=[VMEM]...  23.9 us
    pallas_call x1, Pallas kernels, fwd(): pl.pallas_call(fwd_kernel, in_specs=[SMEM] + [VMEM] * 4, out_specs=[VMEM,...  13.7 us
    all_to_all x1, starting transfers between devices, on_device(): lax.all_to_all(pieces.reshape(64, 16, WIDE), PLANE, 0, 0, tiled=True)  11.5 us
    ppermute x9, starting transfers between devices, along(): return lax.ppermute(x, 'head', [(i, (i + k) % 4) for i in range(4)])  9.99 us
    ppermute x9, waiting for transfers between devices, along(): return lax.ppermute(x, 'head', [(i, (i + k) % 4) for i in range(4)])  4.39 us
  transfers between devices with their start and end apart: 12, of which 5 were waited for; matrix products, arithmetic and copies ran while one was open for 3% of the time, Pallas kernels for 25%

profile of v5, /device:TPU:0, one launch (start us, length us, event | category | flops | bytes accessed | tf_op | source)
XLA Modules:
  0.0 149.9 jit_solution(8499301737869354342)
XLA Ops:
  0.6 2.7 %pack.1 = bf16[4,16,16,1152]{3,2,1,0:T(8,128)(2,1)} custom-call(bf16[128,1024]{1,0:T(8,128)(2,1)} %bitcast.19, bf16[128,256]{1,0:T(8,128)(2,1)} %bitcast.21, bf16[128,256]{1,0:T(8,128)(2,1)} %bitcast.22, bf16[128,1024]{1,0:T(8,128)(2,1)} %bitcast.20), custom_call_target="tpu_custom_call" | custom-call | tf_op jit(solution)/shard_map/pack/pallas_call | solution.py:296
  3.3 0.0 copy-start
  3.3 11.5 %all-to-all-start = ((bf16[64,16,1152]{2,1,0:T(8,128)(2,1)}), bf16[64,16,1152]{2,1,0:T(8,128)(2,1)S(1)}, u32[]{:S(2)}, u32[]{:S(2)}) async-start(bf16[64,16,1152]{2,1,0:T(8,128)(2,1)} %bitcast.18), calls=%async_computation | async-start | bytes 4718592 | tf_op jit(solution)/shard_map/all_to_all | solution.py:402
  14.9 0.1 and.222
  15.0 0.1 and.227
  15.1 0.1 add.207
  15.2 0.1 sub.124
  15.2 0.1 add_add_fusion
  15.3 0.1 add.204
  15.4 0.1 add.205
  15.5 0.0 copy-done
  15.5 0.1 select_reduce_fusion.3
  15.6 0.1 select_reduce_fusion.2
  15.7 0.2 fusion.4
  15.9 0.1 ge.95
  16.0 0.1 and.226
  16.1 0.1 convert_reduce_fusion
  16.2 0.1 convert_reduce_fusion.1
  16.4 0.2 select_reduce_fusion.1
  16.5 30.7 %all-to-all-done = bf16[64,16,1152]{2,1,0:T(8,128)(2,1)S(1)} async-done(((bf16[64,16,1152]{2,1,0:T(8,128)(2,1)}), bf16[64,16,1152]{2,1,0:T(8,128)(2,1)S(1)}, u32[]{:S(2)}, u32[]{:S(2)}) %all-to-all-start) | async-done | bytes 2359328 | tf_op jit(solution)/shard_map/all_to_all | solution.py:402
  47.2 1.1 slice.18
  48.4 0.0 collective-permute-start
  48.4 0.1 tile.18
  48.5 0.1 tile.16
  48.6 0.7 convert_reduce_fusion.3
  49.3 0.6 compare_select_fusion.1
  50.0 0.7 compare_select_fusion
  50.7 1.2 collective-permute-start.3
  51.9 1.0 collective-permute-start.2
  52.9 0.5 collective-permute-start.1
  53.4 0.0 collective-permute-done.oth_ref
  53.4 0.1 broadcast_in_dim.85.kpos_ref
  53.5 13.7 %fwd.1 = (f32[16,128,256]{2,1,0:T(8,128)S(1)}, f32[16,4,256]{2,1,0:T(4,128)S(1)}) custom-call(s32[2,160]{1,0:T(2,128)S(1)} %pad_add_fusion.1.steps, s32[17,2,256]{2,1,0:T(2,128)S(1)} %pad_add_fusion.pos_ref, s32[256,128]{1,0:T(8,128)S(1)} %broadcast_in_dim.85.kpos_ref, bf16[4,16,16,1152]{3,2,1,0:T(8,128)(2,1)S(1)} %bitcast.16, ...), custom_call_target="tpu_custom_call" | custom-call | flops 15000000512 | bytes 8388608 | tf_op jit(solution)/shard_map/fwd/pallas_call | solution.py:217
  67.3 0.0 collective-permute-done.3.do3_ref
  67.3 0.0 collective-permute-done.2.do2_ref
  67.3 0.2 collective-permute-done.1.do1_ref
  67.5 0.6 delta.1.st0_ref
  68.0 2.6 %collective-permute-start.6 = (f32[16,2,256]{2,1,0:T(2,128)S(1)}, f32[16,2,256]{2,1,0:T(2,128)S(1)}, u32[]{:S(2)}, u32[]{:S(2)}) collective-permute-start(f32[16,2,256]{2,1,0:T(2,128)S(1)} %delta.1.st0_ref), channel_id=1, source_target_pairs={{0,96},{32,0},{64,32},{96,64},{1,97},{33,1},{65,33},{97,65},{2,98}... | collective-permute-start | bytes 98312 | tf_op jit(solution)/shard_map/ppermute | solution.py:406
  70.6 1.3 collective-permute-start.5
  72.0 0.9 collective-permute-start.4
  72.9 0.0 collective-permute-done.6.st3_ref
  72.9 3.1 %collective-permute-done.5.st2_ref = f32[16,2,256]{2,1,0:T(2,128)S(1)} collective-permute-done((f32[16,2,256]{2,1,0:T(2,128)S(1)}, f32[16,2,256]{2,1,0:T(2,128)S(1)}, u32[]{:S(2)}, u32[]{:S(2)}) %collective-permute-start.5) | collective-permute-done | bytes 32800 | tf_op jit(solution)/shard_map/ppermute | solution.py:406
  76.0 1.1 collective-permute-done.4.st1_ref
  77.1 1.0 scale.1
  78.1 0.4 collective-permute-start.7
  78.5 1.4 collective-permute-start.8
  79.9 0.6 collective-permute-start.9
  80.6 23.9 %bwd.1 = (bf16[4,16,16,1152]{3,2,1,0:T(8,128)(2,1)S(1)}, bf16[4,16,16,512]{3,2,1,0:T(8,128)(2,1)S(1)}) custom-call(s32[2,160]{1,0:T(2,128)S(1)} %pad_add_fusion.1.steps, s32[17,2,256]{2,1,0:T(2,128)S(1)} %pad_add_fusion.pos_ref, s32[256,128]{1,0:T(8,128)S(1)} %broadcast_in_dim.85.kpos_ref, f32[17,2,256]{2,1,0:T(2,128)S(1)} %get-tuple-element.21.stat_ref, ...), custom_call_target="tpu_custom_call" | custom-call | flops 24999999488 | bytes 8388608 | tf_op jit(solution)/shard_map/bwd/pallas_call | solution.py:249
  104.5 0.0 collective-permute-done.7.o1_ref
  104.5 0.0 collective-permute-done.8.o2_ref
  104.5 0.0 collective-permute-done.9.o3_ref
  104.5 0.2 gather_parts.1
  104.7 0.1 collective-permute-start.10
  104.8 2.6 %collective-permute-done.10.other_ref = bf16[4,16,16,512]{3,2,1,0:T(8,128)(2,1)S(1)} collective-permute-done((bf16[4,16,16,512]{3,2,1,0:T(8,128)(2,1)S(1)}, bf16[4,16,16,512]{3,2,1,0:T(8,128)(2,1)S(1)}, u32[]{:S(2)}, u32[]{:S(2)}) %collective-permute-start.10) | collective-permute-done | bytes 1048608 | tf_op jit(solution)/shard_map/ppermute | solution.py:416
  107.4 0.5 add_parts.1
  108.0 41.0 %all_to_all.10.in_ref = bf16[64,16,1152]{2,1,0:T(8,128)(2,1)S(1)} all-to-all(bf16[64,16,1152]{2,1,0:T(8,128)(2,1)S(1)} %bitcast.13), channel_id=1, replica_groups=mesh['head'=4,'inner'=8,'zl'=2,'core'=2] {'head','inner','zl'}, dimensions={0} | all-to-all | bytes 4718592 | tf_op jit(solution)/shard_map/all_to_all | solution.py:417
  149.0 1.0 sum_pieces.1
  (19 shorter events, 0.2 us)
Async XLA Ops:
  3.3 12.2 %copy-start = (s32[4]{0:T(128)S(1)}, s32[4]{0:T(128)}, u32[]{:S(2)}) copy-start(s32[4]{0:T(128)} %param.9) | copy-start | bytes 52
  3.3 43.9 %all-to-all-start = ((bf16[64,16,1152]{2,1,0:T(8,128)(2,1)}), bf16[64,16,1152]{2,1,0:T(8,128)(2,1)S(1)}, u32[]{:S(2)}, u32[]{:S(2)}) async-start(bf16[64,16,1152]{2,1,0:T(8,128)(2,1)} %bitcast.18), calls=%async_computation | async-start | bytes 4718592 | tf_op jit(solution)/shard_map/all_to_all | solution.py:402
  48.4 5.1 %collective-permute-start = (bf16[4,16,16,512]{3,2,1,0:T(8,128)(2,1)}, bf16[4,16,16,512]{3,2,1,0:T(8,128)(2,1)S(1)}, u32[]{:S(2)}, u32[]{:S(2)}) collective-permute-start(bf16[4,16,16,512]{3,2,1,0:T(8,128)(2,1)} %slice.18), channel_id=1, source_target_pairs={{0,1},{1,0},{2,3},{3,2},{4,5},{5,4},{6,7},{7,6},{8,9},{9,8},{10,11... | collective-permute-start | bytes 3145736 | tf_op jit(solution)/shard_map/ppermute | solution.py:403
  50.7 16.5 %collective-permute-start.3 = (bf16[4,16,16,128]{3,2,1,0:T(8,128)(2,1)S(1)}, bf16[4,16,16,128]{3,2,1,0:T(8,128)(2,1)S(1)}, u32[]{:S(2)}, u32[]{:S(2)}) collective-permute-start(bf16[4,16,16,128]{3,2,1,0:T(8,128)(2,1)S(1)} %slice.19.do0_ref), channel_id=1, source_target_pairs={{0,96},{32,0},{64,32},{96,64},{1,97},{33,1},{65,33},{97,65},{2,98}... | collective-permute-start | bytes 786440 | tf_op jit(solution)/shard_map/ppermute | solution.py:406
  51.9 15.4 %collective-permute-start.2 = (bf16[4,16,16,128]{3,2,1,0:T(8,128)(2,1)S(1)}, bf16[4,16,16,128]{3,2,1,0:T(8,128)(2,1)S(1)}, u32[]{:S(2)}, u32[]{:S(2)}) collective-permute-start(bf16[4,16,16,128]{3,2,1,0:T(8,128)(2,1)S(1)} %slice.19.do0_ref), channel_id=1, source_target_pairs={{0,64},{32,96},{64,0},{96,32},{1,65},{33,97},{65,1},{97,33},{2,66}... | collective-permute-start | bytes 786440 | tf_op jit(solution)/shard_map/ppermute | solution.py:406
  52.9 14.6 %collective-permute-start.1 = (bf16[4,16,16,128]{3,2,1,0:T(8,128)(2,1)S(1)}, bf16[4,16,16,128]{3,2,1,0:T(8,128)(2,1)S(1)}, u32[]{:S(2)}, u32[]{:S(2)}) collective-permute-start(bf16[4,16,16,128]{3,2,1,0:T(8,128)(2,1)S(1)} %slice.19.do0_ref), channel_id=1, source_target_pairs={{0,32},{32,64},{64,96},{96,0},{1,33},{33,65},{65,97},{97,1},{2,34}... | collective-permute-start | bytes 786440 | tf_op jit(solution)/shard_map/ppermute | solution.py:406
  68.0 4.9 %collective-permute-start.6 = (f32[16,2,256]{2,1,0:T(2,128)S(1)}, f32[16,2,256]{2,1,0:T(2,128)S(1)}, u32[]{:S(2)}, u32[]{:S(2)}) collective-permute-start(f32[16,2,256]{2,1,0:T(2,128)S(1)} %delta.1.st0_ref), channel_id=1, source_target_pairs={{0,96},{32,0},{64,32},{96,64},{1,97},{33,1},{65,33},{97,65},{2,98}... | collective-permute-start | bytes 98312 | tf_op jit(solution)/shard_map/ppermute | solution.py:406
  70.6 5.4 %collective-permute-start.5 = (f32[16,2,256]{2,1,0:T(2,128)S(1)}, f32[16,2,256]{2,1,0:T(2,128)S(1)}, u32[]{:S(2)}, u32[]{:S(2)}) collective-permute-start(f32[16,2,256]{2,1,0:T(2,128)S(1)} %delta.1.st0_ref), channel_id=1, source_target_pairs={{0,64},{32,96},{64,0},{96,32},{1,65},{33,97},{65,1},{97,33},{2,66}... | collective-permute-start | bytes 98312 | tf_op jit(solution)/shard_map/ppermute | solution.py:406
  72.0 5.1 %collective-permute-start.4 = (f32[16,2,256]{2,1,0:T(2,128)S(1)}, f32[16,2,256]{2,1,0:T(2,128)S(1)}, u32[]{:S(2)}, u32[]{:S(2)}) collective-permute-start(f32[16,2,256]{2,1,0:T(2,128)S(1)} %delta.1.st0_ref), channel_id=1, source_target_pairs={{0,32},{32,64},{64,96},{96,0},{1,33},{33,65},{65,97},{97,1},{2,34}... | collective-permute-start | bytes 98312 | tf_op jit(solution)/shard_map/ppermute | solution.py:406
  78.1 26.4 %collective-permute-start.7 = (bf16[4,16,16,128]{3,2,1,0:T(8,128)(2,1)S(1)}, bf16[4,16,16,128]{3,2,1,0:T(8,128)(2,1)S(1)}, u32[]{:S(2)}, u32[]{:S(2)}) collective-permute-start(bf16[4,16,16,128]{3,2,1,0:T(8,128)(2,1)S(1)} %get-tuple-element.25), channel_id=1, source_target_pairs={{0,96},{32,0},{64,32},{96,64},{1,97},{33,1},{65,33},{97,65},{2,98}... | collective-permute-start | bytes 786440 | tf_op jit(solution)/shard_map/ppermute | solution.py:406
  78.5 26.0 %collective-permute-start.8 = (bf16[4,16,16,128]{3,2,1,0:T(8,128)(2,1)S(1)}, bf16[4,16,16,128]{3,2,1,0:T(8,128)(2,1)S(1)}, u32[]{:S(2)}, u32[]{:S(2)}) collective-permute-start(bf16[4,16,16,128]{3,2,1,0:T(8,128)(2,1)S(1)} %get-tuple-element.26), channel_id=1, source_target_pairs={{0,64},{32,96},{64,0},{96,32},{1,65},{33,97},{65,1},{97,33},{2,66}... | collective-permute-start | bytes 786440 | tf_op jit(solution)/shard_map/ppermute | solution.py:406
  79.9 24.5 %collective-permute-start.9 = (bf16[4,16,16,128]{3,2,1,0:T(8,128)(2,1)S(1)}, bf16[4,16,16,128]{3,2,1,0:T(8,128)(2,1)S(1)}, u32[]{:S(2)}, u32[]{:S(2)}) collective-permute-start(bf16[4,16,16,128]{3,2,1,0:T(8,128)(2,1)S(1)} %get-tuple-element.27), channel_id=1, source_target_pairs={{0,32},{32,64},{64,96},{96,0},{1,33},{33,65},{65,97},{97,1},{2,34}... | collective-permute-start | bytes 786440 | tf_op jit(solution)/shard_map/ppermute | solution.py:406
  104.7 2.7 %collective-permute-start.10 = (bf16[4,16,16,512]{3,2,1,0:T(8,128)(2,1)S(1)}, bf16[4,16,16,512]{3,2,1,0:T(8,128)(2,1)S(1)}, u32[]{:S(2)}, u32[]{:S(2)}) collective-permute-start(bf16[4,16,16,512]{3,2,1,0:T(8,128)(2,1)S(1)} %get-tuple-element.28), channel_id=1, source_target_pairs={{0,1},{1,0},{2,3},{3,2},{4,5},{5,4},{6,7},{7,6},{8,9},{9,8},{10,11... | collective-permute-start | bytes 3145736 | tf_op jit(solution)/shard_map/ppermute | solution.py:416
